TPU v7x, 256 devices: a whole 4x4x8 slice. The times are simulated.
256 devices in a mesh: tm: 32 (over x, z_lo, core), tensor: 8 (over y, z_hi).
Axes of the slice: x: 4, y: 4, z: 8 (z_hi: 2, z_lo: 4; z = z_hi * 4 + z_lo), core: 2. Of those that a mesh axis runs over, the one named last changes fastest.
Arguments:
- hidden_state: bfloat16 [32, 384, 3072], P('tm')
- base_latent: float32 [384, 64], P('tensor'), may hold values from -6 to 6
- w_modulation: bfloat16 [256, 9216], replicated, may hold values from -1 to 1
- w_up: bfloat16 [3072, 6144], P('tm', 'tensor'), may hold values from -0.109375 to 0.109375
- w_down: bfloat16 [6144, 3072], P('tensor', 'tm'), may hold values from -0.078125 to 0.078125
- w_out: bfloat16 [3072, 64], replicated, may hold values from -0.109375 to 0.109375
- times: int32 [32], P('tm'), may hold values from 0 to 999
- sched_index: int32 [32], P('tm'), may hold values from 0 to 999
- slide_count: int32 [1], replicated, may hold values from 1 to 31
Outputs:
- new_latents: float32 [32, 384, 64], P('tm', 'tensor')
All inputs are finite; a program needn't handle non-finite values.
Results may differ from a plain program's by a relative error of at most 0.002.
Values may be sent and summed in bfloat16 or wider, within the bound.
A program may use at most 64 MiB of HBM per device.

v0:
```python
import math

import jax
import jax.numpy as jnp
from jax import lax
from jax.sharding import PartitionSpec as P

SCHED = 1000


def carried_in(part, axis, combine, identity):
    place = lax.axis_index(axis)
    gathered = lax.all_gather(part, axis)
    state = jnp.zeros_like(part) + jnp.asarray(identity, part.dtype)

    def one(lap, state):
        return combine(state, lax.dynamic_index_in_dim(gathered, lap, 0, False))

    return lax.fori_loop(0, place, one, state)


def from_behind(value, axis, steps):
    count = lax.axis_size(axis)
    leading, last = (max(0, -steps), min(count, count - steps))
    return lax.ppermute(value, axis, [(source, source + steps) for source in range(leading, last)])


def modulation(times, w_modulation):
    half = w_modulation.shape[0] // 2
    freqs = jnp.exp(-math.log(10000.0) * jnp.arange(half, dtype=jnp.float32) / half)
    angles = times.astype(jnp.float32)[:, None] * freqs[None, :]
    embed = jnp.concatenate([jnp.cos(angles), jnp.sin(angles)], axis=1)
    cond = jax.nn.silu(embed).astype(jnp.bfloat16)
    return jnp.dot(cond, w_modulation, preferred_element_type=jnp.float32)


def body(
    hidden_state, base_latent, w_modulation, w_up, w_down, w_out, times, sched_index, slide_count
):
    width = hidden_state.shape[2]
    mods = modulation(times, w_modulation)[0]
    shift = mods[:width]
    scale = mods[width : 2 * width]
    gate = mods[2 * width :]
    hidden = hidden_state[0]
    values = hidden.astype(jnp.float32)
    center = jnp.mean(values, axis=-1, keepdims=True)
    spread = jnp.mean((values - center) ** 2, axis=-1, keepdims=True)
    normed = ((values - center) * lax.rsqrt(spread + 1e-06) * (1.0 + scale) + shift).astype(
        jnp.bfloat16
    )
    pre_act = jnp.dot(
        normed, lax.all_gather(w_up, "tm", axis=0, tiled=True), preferred_element_type=jnp.float32
    )
    active = jax.nn.gelu(pre_act, approximate=True).astype(jnp.bfloat16)
    mixed = jnp.dot(
        active, lax.all_gather(w_down, "tm", axis=1, tiled=True), preferred_element_type=jnp.float32
    )
    rank = lax.axis_index("tensor")
    share_width = width // lax.axis_size("tensor")
    offset = rank * share_width
    hidden_share = lax.dynamic_slice_in_dim(hidden, offset, share_width, 1)
    head_share = lax.dynamic_slice_in_dim(w_out, offset, share_width, 0)
    term = jnp.dot(hidden_share, head_share, preferred_element_type=jnp.float32)
    term = term + jnp.dot(gate * mixed, w_out.astype(jnp.float32), precision=lax.Precision.HIGHEST)
    drift = lax.psum_scatter(term, "tensor", scatter_dimension=0, tiled=True)
    step_size = 0.1 + 0.3 * sched_index.astype(jnp.float32)[0] / SCHED
    weighted = step_size * drift

    def combine(earlier, later):
        return earlier + later

    before = carried_in(weighted, "tm", combine, jnp.zeros_like(weighted))
    reached = base_latent + before + weighted
    window = lax.axis_size("tm")
    place = lax.axis_index("tm")
    advance = slide_count[0] - 1

    def advance_once(count, current):
        moved = from_behind(current, "tm", -1)
        taken = jnp.logical_and(count < advance, place < window - 1)
        return jnp.where(taken, moved, current)

    result = lax.fori_loop(0, window - 1, advance_once, reached)[None]
    return result


def solution(mesh):
    placed = (
        P("tm", None, None),
        P("tensor", None),
        P(),
        P("tm", "tensor"),
        P("tensor", "tm"),
        P(),
        P("tm"),
        P("tm"),
        P(),
    )
    return jax.shard_map(
        body, mesh=mesh, in_specs=placed, out_specs=P("tm", "tensor", None), check_vma=False
    )
```

profile of v0, /device:TPU:97, one launch (start us, length us, event | category | flops | bytes accessed | tf_op | source)
XLA Modules:
  0.0 525.9 jit_solution(5123304680314478707)
XLA Ops:
  8.8 2.2 convert_reduce_fusion
  11.0 2.4 fusion.3
  13.4 3.1 fusion.47
  16.5 57.6 %all-gather.4.cloned.1.call-done = bf16[3072,768]{1,0:T(8,128)(2,1)} async-done(((bf16[96,768]{1,0:T(8,128)(2,1)}), bf16[3072,768]{1,0:T(8,128)(2,1)}) %all-gather.4.cloned.1.call-update) | async-done | bytes 4718608 | tf_op jit(solution)/shard_map/all_gather | solution.py:53
  74.1 64.4 %all-gather.6.cloned.1.call-done = bf16[768,3072]{0,1:T(8,128)(2,1)} async-done(((bf16[768,96]{0,1:T(8,128)(2,1)}), bf16[768,3072]{0,1:T(8,128)(2,1)}) %all-gather.6.cloned.1.call-update) | async-done | bytes 4718608 | tf_op jit(solution)/shard_map/all_gather | solution.py:57
  138.5 11.1 %fusion.29 = f32[384,3072]{1,0:T(8,128)} fusion(bf16[768,3072]{0,1:T(8,128)(2,1)} %all-gather.6.cloned.1.call-done, bf16[3072,768]{1,0:T(8,128)(2,1)} %all-gather.4.cloned.1.call-done, bf16[1,384,3072]{2,1,0:T(8,128)(2,1)S(1)} %copy-done.1, f32[3072]{0:T(1024)S(1)} %get-tuple-element.154, f32[3072]{0:T(1024)S(1)} %get-tuple-element.155, ...), kind=kOutput, calls=%fused_computation.29 | convolution fusion | flops 3633610752 | bytes 16542720 | tf_op jit(solution)/shard_map/dot_general | solution.py:56
  149.6 4.7 fusion.7
  156.5 76.7 %reduce-scatter.2.cloned.1.call-done = f32[48,64]{1,0:T(8,128)} async-done(((f32[384,64]{1,0:T(8,128)}), f32[48,64]{1,0:T(8,128)}) %reduce-scatter.2.cloned.1.call-update) | async-done | bytes 12304 | tf_op jit(solution)/shard_map/reduce_scatter | solution.py:66
  234.0 40.8 %all-gather = f32[1536,64]{1,0:T(8,128)S(1)} all-gather(f32[48,64]{1,0:T(8,128)S(1)} %broadcast_multiply_fusion), channel_id=2, replica_groups=mesh['tm'=32,'tensor'=8] {'tm'}, dimensions={0}, use_global_device_ids=true | all-gather | bytes 405504 | tf_op jit(solution)/shard_map/all_gather | solution.py:13
  275.8 243.0 %while.26 = (s32[]{:T(128)}, f32[48,64]{1,0:T(8,128)S(1)}, s32[]{:T(128)}, pred[]{:T(512)}, s32[]{:T(128)}) while((s32[]{:T(128)}, f32[48,64]{1,0:T(8,128)S(1)}, s32[]{:T(128)}, pred[]{:T(512)}, s32[]{:T(128)}) %tuple.54), condition=%wide.region_6.7_spmd, body=%wide.region_5.6_spmd.sunk | while | flops 3076 | bytes 86130 | solution.py:84
  275.8 2.0 collective-permute-start
  277.8 5.8 %collective-permute-done = f32[48,64]{1,0:T(8,128)S(1)} collective-permute-done((f32[48,64]{1,0:T(8,128)S(1)}, f32[48,64]{1,0:T(8,128)S(1)}, u32[]{:S(2)}, u32[]{:S(2)}) %collective-permute-start) | collective-permute-done | bytes 12320 | tf_op jit(solution)/shard_map/while/body/eval_jaxpr/ppermute | solution.py:25
  285.6 5.9 %collective-permute-done = f32[48,64]{1,0:T(8,128)S(1)} collective-permute-done((f32[48,64]{1,0:T(8,128)S(1)}, f32[48,64]{1,0:T(8,128)S(1)}, u32[]{:S(2)}, u32[]{:S(2)}) %collective-permute-start) | collective-permute-done | bytes 12320 | tf_op jit(solution)/shard_map/while/body/eval_jaxpr/ppermute | solution.py:25
  291.5 1.9 collective-permute-start
  293.4 5.9 %collective-permute-done = f32[48,64]{1,0:T(8,128)S(1)} collective-permute-done((f32[48,64]{1,0:T(8,128)S(1)}, f32[48,64]{1,0:T(8,128)S(1)}, u32[]{:S(2)}, u32[]{:S(2)}) %collective-permute-start) | collective-permute-done | bytes 12320 | tf_op jit(solution)/shard_map/while/body/eval_jaxpr/ppermute | solution.py:25
  301.2 5.9 %collective-permute-done = f32[48,64]{1,0:T(8,128)S(1)} collective-permute-done((f32[48,64]{1,0:T(8,128)S(1)}, f32[48,64]{1,0:T(8,128)S(1)}, u32[]{:S(2)}, u32[]{:S(2)}) %collective-permute-start) | collective-permute-done | bytes 12320 | tf_op jit(solution)/shard_map/while/body/eval_jaxpr/ppermute | solution.py:25
  309.1 5.9 %collective-permute-done = f32[48,64]{1,0:T(8,128)S(1)} collective-permute-done((f32[48,64]{1,0:T(8,128)S(1)}, f32[48,64]{1,0:T(8,128)S(1)}, u32[]{:S(2)}, u32[]{:S(2)}) %collective-permute-start) | collective-permute-done | bytes 12320 | tf_op jit(solution)/shard_map/while/body/eval_jaxpr/ppermute | solution.py:25
  316.9 5.9 %collective-permute-done = f32[48,64]{1,0:T(8,128)S(1)} collective-permute-done((f32[48,64]{1,0:T(8,128)S(1)}, f32[48,64]{1,0:T(8,128)S(1)}, u32[]{:S(2)}, u32[]{:S(2)}) %collective-permute-start) | collective-permute-done | bytes 12320 | tf_op jit(solution)/shard_map/while/body/eval_jaxpr/ppermute | solution.py:25
  322.8 1.9 collective-permute-start
  324.7 5.9 %collective-permute-done = f32[48,64]{1,0:T(8,128)S(1)} collective-permute-done((f32[48,64]{1,0:T(8,128)S(1)}, f32[48,64]{1,0:T(8,128)S(1)}, u32[]{:S(2)}, u32[]{:S(2)}) %collective-permute-start) | collective-permute-done | bytes 12320 | tf_op jit(solution)/shard_map/while/body/eval_jaxpr/ppermute | solution.py:25
  332.6 5.9 %collective-permute-done = f32[48,64]{1,0:T(8,128)S(1)} collective-permute-done((f32[48,64]{1,0:T(8,128)S(1)}, f32[48,64]{1,0:T(8,128)S(1)}, u32[]{:S(2)}, u32[]{:S(2)}) %collective-permute-start) | collective-permute-done | bytes 12320 | tf_op jit(solution)/shard_map/while/body/eval_jaxpr/ppermute | solution.py:25
  340.4 5.9 %collective-permute-done = f32[48,64]{1,0:T(8,128)S(1)} collective-permute-done((f32[48,64]{1,0:T(8,128)S(1)}, f32[48,64]{1,0:T(8,128)S(1)}, u32[]{:S(2)}, u32[]{:S(2)}) %collective-permute-start) | collective-permute-done | bytes 12320 | tf_op jit(solution)/shard_map/while/body/eval_jaxpr/ppermute | solution.py:25
  346.3 1.9 collective-permute-start
  348.3 5.9 %collective-permute-done = f32[48,64]{1,0:T(8,128)S(1)} collective-permute-done((f32[48,64]{1,0:T(8,128)S(1)}, f32[48,64]{1,0:T(8,128)S(1)}, u32[]{:S(2)}, u32[]{:S(2)}) %collective-permute-start) | collective-permute-done | bytes 12320 | tf_op jit(solution)/shard_map/while/body/eval_jaxpr/ppermute | solution.py:25
  354.2 1.9 collective-permute-start
  356.1 5.9 %collective-permute-done = f32[48,64]{1,0:T(8,128)S(1)} collective-permute-done((f32[48,64]{1,0:T(8,128)S(1)}, f32[48,64]{1,0:T(8,128)S(1)}, u32[]{:S(2)}, u32[]{:S(2)}) %collective-permute-start) | collective-permute-done | bytes 12320 | tf_op jit(solution)/shard_map/while/body/eval_jaxpr/ppermute | solution.py:25
  363.9 5.9 %collective-permute-done = f32[48,64]{1,0:T(8,128)S(1)} collective-permute-done((f32[48,64]{1,0:T(8,128)S(1)}, f32[48,64]{1,0:T(8,128)S(1)}, u32[]{:S(2)}, u32[]{:S(2)}) %collective-permute-start) | collective-permute-done | bytes 12320 | tf_op jit(solution)/shard_map/while/body/eval_jaxpr/ppermute | solution.py:25
  371.8 5.9 %collective-permute-done = f32[48,64]{1,0:T(8,128)S(1)} collective-permute-done((f32[48,64]{1,0:T(8,128)S(1)}, f32[48,64]{1,0:T(8,128)S(1)}, u32[]{:S(2)}, u32[]{:S(2)}) %collective-permute-start) | collective-permute-done | bytes 12320 | tf_op jit(solution)/shard_map/while/body/eval_jaxpr/ppermute | solution.py:25
  377.7 1.9 collective-permute-start
  379.6 5.9 %collective-permute-done = f32[48,64]{1,0:T(8,128)S(1)} collective-permute-done((f32[48,64]{1,0:T(8,128)S(1)}, f32[48,64]{1,0:T(8,128)S(1)}, u32[]{:S(2)}, u32[]{:S(2)}) %collective-permute-start) | collective-permute-done | bytes 12320 | tf_op jit(solution)/shard_map/while/body/eval_jaxpr/ppermute | solution.py:25
  385.5 1.9 collective-permute-start
  387.5 5.9 %collective-permute-done = f32[48,64]{1,0:T(8,128)S(1)} collective-permute-done((f32[48,64]{1,0:T(8,128)S(1)}, f32[48,64]{1,0:T(8,128)S(1)}, u32[]{:S(2)}, u32[]{:S(2)}) %collective-permute-start) | collective-permute-done | bytes 12320 | tf_op jit(solution)/shard_map/while/body/eval_jaxpr/ppermute | solution.py:25
  395.3 5.9 %collective-permute-done = f32[48,64]{1,0:T(8,128)S(1)} collective-permute-done((f32[48,64]{1,0:T(8,128)S(1)}, f32[48,64]{1,0:T(8,128)S(1)}, u32[]{:S(2)}, u32[]{:S(2)}) %collective-permute-start) | collective-permute-done | bytes 12320 | tf_op jit(solution)/shard_map/while/body/eval_jaxpr/ppermute | solution.py:25
  403.1 5.9 %collective-permute-done = f32[48,64]{1,0:T(8,128)S(1)} collective-permute-done((f32[48,64]{1,0:T(8,128)S(1)}, f32[48,64]{1,0:T(8,128)S(1)}, u32[]{:S(2)}, u32[]{:S(2)}) %collective-permute-start) | collective-permute-done | bytes 12320 | tf_op jit(solution)/shard_map/while/body/eval_jaxpr/ppermute | solution.py:25
  411.0 5.9 %collective-permute-done = f32[48,64]{1,0:T(8,128)S(1)} collective-permute-done((f32[48,64]{1,0:T(8,128)S(1)}, f32[48,64]{1,0:T(8,128)S(1)}, u32[]{:S(2)}, u32[]{:S(2)}) %collective-permute-start) | collective-permute-done | bytes 12320 | tf_op jit(solution)/shard_map/while/body/eval_jaxpr/ppermute | solution.py:25
  418.8 5.9 %collective-permute-done = f32[48,64]{1,0:T(8,128)S(1)} collective-permute-done((f32[48,64]{1,0:T(8,128)S(1)}, f32[48,64]{1,0:T(8,128)S(1)}, u32[]{:S(2)}, u32[]{:S(2)}) %collective-permute-start) | collective-permute-done | bytes 12320 | tf_op jit(solution)/shard_map/while/body/eval_jaxpr/ppermute | solution.py:25
  426.6 5.9 %collective-permute-done = f32[48,64]{1,0:T(8,128)S(1)} collective-permute-done((f32[48,64]{1,0:T(8,128)S(1)}, f32[48,64]{1,0:T(8,128)S(1)}, u32[]{:S(2)}, u32[]{:S(2)}) %collective-permute-start) | collective-permute-done | bytes 12320 | tf_op jit(solution)/shard_map/while/body/eval_jaxpr/ppermute | solution.py:25
  434.5 5.9 %collective-permute-done = f32[48,64]{1,0:T(8,128)S(1)} collective-permute-done((f32[48,64]{1,0:T(8,128)S(1)}, f32[48,64]{1,0:T(8,128)S(1)}, u32[]{:S(2)}, u32[]{:S(2)}) %collective-permute-start) | collective-permute-done | bytes 12320 | tf_op jit(solution)/shard_map/while/body/eval_jaxpr/ppermute | solution.py:25
  442.3 5.9 %collective-permute-done = f32[48,64]{1,0:T(8,128)S(1)} collective-permute-done((f32[48,64]{1,0:T(8,128)S(1)}, f32[48,64]{1,0:T(8,128)S(1)}, u32[]{:S(2)}, u32[]{:S(2)}) %collective-permute-start) | collective-permute-done | bytes 12320 | tf_op jit(solution)/shard_map/while/body/eval_jaxpr/ppermute | solution.py:25
  450.2 5.9 %collective-permute-done = f32[48,64]{1,0:T(8,128)S(1)} collective-permute-done((f32[48,64]{1,0:T(8,128)S(1)}, f32[48,64]{1,0:T(8,128)S(1)}, u32[]{:S(2)}, u32[]{:S(2)}) %collective-permute-start) | collective-permute-done | bytes 12320 | tf_op jit(solution)/shard_map/while/body/eval_jaxpr/ppermute | solution.py:25
  458.0 5.9 %collective-permute-done = f32[48,64]{1,0:T(8,128)S(1)} collective-permute-done((f32[48,64]{1,0:T(8,128)S(1)}, f32[48,64]{1,0:T(8,128)S(1)}, u32[]{:S(2)}, u32[]{:S(2)}) %collective-permute-start) | collective-permute-done | bytes 12320 | tf_op jit(solution)/shard_map/while/body/eval_jaxpr/ppermute | solution.py:25
  465.8 5.9 %collective-permute-done = f32[48,64]{1,0:T(8,128)S(1)} collective-permute-done((f32[48,64]{1,0:T(8,128)S(1)}, f32[48,64]{1,0:T(8,128)S(1)}, u32[]{:S(2)}, u32[]{:S(2)}) %collective-permute-start) | collective-permute-done | bytes 12320 | tf_op jit(solution)/shard_map/while/body/eval_jaxpr/ppermute | solution.py:25
  473.7 5.9 %collective-permute-done = f32[48,64]{1,0:T(8,128)S(1)} collective-permute-done((f32[48,64]{1,0:T(8,128)S(1)}, f32[48,64]{1,0:T(8,128)S(1)}, u32[]{:S(2)}, u32[]{:S(2)}) %collective-permute-start) | collective-permute-done | bytes 12320 | tf_op jit(solution)/shard_map/while/body/eval_jaxpr/ppermute | solution.py:25
  481.5 5.9 %collective-permute-done = f32[48,64]{1,0:T(8,128)S(1)} collective-permute-done((f32[48,64]{1,0:T(8,128)S(1)}, f32[48,64]{1,0:T(8,128)S(1)}, u32[]{:S(2)}, u32[]{:S(2)}) %collective-permute-start) | collective-permute-done | bytes 12320 | tf_op jit(solution)/shard_map/while/body/eval_jaxpr/ppermute | solution.py:25
  489.3 5.9 %collective-permute-done = f32[48,64]{1,0:T(8,128)S(1)} collective-permute-done((f32[48,64]{1,0:T(8,128)S(1)}, f32[48,64]{1,0:T(8,128)S(1)}, u32[]{:S(2)}, u32[]{:S(2)}) %collective-permute-start) | collective-permute-done | bytes 12320 | tf_op jit(solution)/shard_map/while/body/eval_jaxpr/ppermute | solution.py:25
  497.2 5.9 %collective-permute-done = f32[48,64]{1,0:T(8,128)S(1)} collective-permute-done((f32[48,64]{1,0:T(8,128)S(1)}, f32[48,64]{1,0:T(8,128)S(1)}, u32[]{:S(2)}, u32[]{:S(2)}) %collective-permute-start) | collective-permute-done | bytes 12320 | tf_op jit(solution)/shard_map/while/body/eval_jaxpr/ppermute | solution.py:25
  505.0 5.9 %collective-permute-done = f32[48,64]{1,0:T(8,128)S(1)} collective-permute-done((f32[48,64]{1,0:T(8,128)S(1)}, f32[48,64]{1,0:T(8,128)S(1)}, u32[]{:S(2)}, u32[]{:S(2)}) %collective-permute-start) | collective-permute-done | bytes 12320 | tf_op jit(solution)/shard_map/while/body/eval_jaxpr/ppermute | solution.py:25
  512.9 5.9 %collective-permute-done = f32[48,64]{1,0:T(8,128)S(1)} collective-permute-done((f32[48,64]{1,0:T(8,128)S(1)}, f32[48,64]{1,0:T(8,128)S(1)}, u32[]{:S(2)}, u32[]{:S(2)}) %collective-permute-start) | collective-permute-done | bytes 12320 | tf_op jit(solution)/shard_map/while/body/eval_jaxpr/ppermute | solution.py:25
  (87 shorter events, 50.9 us)
Async XLA Ops:
  6.5 143.1 %copy-start = (bf16[3072,64]{0,1:T(8,128)(2,1)S(1)}, bf16[3072,64]{0,1:T(8,128)(2,1)}, u32[]{:S(2)}) copy-start(bf16[3072,64]{0,1:T(8,128)(2,1)} %param.18) | copy-start | bytes 1179652
  6.5 67.5 %all-gather.4.cloned.1.call-start = ((), (), s32[]{:S(2)}) async-start(), calls=%async_computation.1 | async-start | bytes 4866048 | tf_op jit(solution)/shard_map/all_gather | solution.py:53
  7.3 131.3 %all-gather.6.cloned.1.call-start = ((), (), s32[]{:S(2)}) async-start(), calls=%async_computation.2 | async-start | bytes 4866048 | tf_op jit(solution)/shard_map/all_gather | solution.py:57
  8.0 225.2 %reduce-scatter.2.cloned.1.call-start = ((), (), s32[]{:S(2)}) async-start(), calls=%async_computation.3 | async-start | bytes 221184 | tf_op jit(solution)/shard_map/reduce_scatter | solution.py:66
  8.8 129.7 %copy-start.1 = (bf16[1,384,3072]{2,1,0:T(8,128)(2,1)S(1)}, bf16[1,384,3072]{2,1,0:T(8,128)(2,1)}, u32[]{:S(2)}) copy-start(bf16[1,384,3072]{2,1,0:T(8,128)(2,1)} %param.13) | copy-start | bytes 7077892
  149.6 125.4 %copy-start.3 = (f32[48,64]{1,0:T(8,128)S(1)}, f32[48,64]{1,0:T(8,128)}, u32[]{:S(2)}) copy-start(f32[48,64]{1,0:T(8,128)} %param.14) | copy-start | bytes 36868
  275.8 7.8 %collective-permute-start = (f32[48,64]{1,0:T(8,128)S(1)}, f32[48,64]{1,0:T(8,128)S(1)}, u32[]{:S(2)}, u32[]{:S(2)}) collective-permute-start(f32[48,64]{1,0:T(8,128)S(1)} %get-tuple-element.236), channel_id=1, source_target_pairs={{8,0},{16,8},{24,16},{32,24},{40,32},{48,40},{56,48},{64,56},{72,6... | collective-permute-start | bytes 36872 | tf_op jit(solution)/shard_map/while/body/eval_jaxpr/ppermute | solution.py:25
  283.6 7.8 %collective-permute-start = (f32[48,64]{1,0:T(8,128)S(1)}, f32[48,64]{1,0:T(8,128)S(1)}, u32[]{:S(2)}, u32[]{:S(2)}) collective-permute-start(f32[48,64]{1,0:T(8,128)S(1)} %get-tuple-element.236), channel_id=1, source_target_pairs={{8,0},{16,8},{24,16},{32,24},{40,32},{48,40},{56,48},{64,56},{72,6... | collective-permute-start | bytes 36872 | tf_op jit(solution)/shard_map/while/body/eval_jaxpr/ppermute | solution.py:25
  291.5 7.8 %collective-permute-start = (f32[48,64]{1,0:T(8,128)S(1)}, f32[48,64]{1,0:T(8,128)S(1)}, u32[]{:S(2)}, u32[]{:S(2)}) collective-permute-start(f32[48,64]{1,0:T(8,128)S(1)} %get-tuple-element.236), channel_id=1, source_target_pairs={{8,0},{16,8},{24,16},{32,24},{40,32},{48,40},{56,48},{64,56},{72,6... | collective-permute-start | bytes 36872 | tf_op jit(solution)/shard_map/while/body/eval_jaxpr/ppermute | solution.py:25
  299.3 7.8 %collective-permute-start = (f32[48,64]{1,0:T(8,128)S(1)}, f32[48,64]{1,0:T(8,128)S(1)}, u32[]{:S(2)}, u32[]{:S(2)}) collective-permute-start(f32[48,64]{1,0:T(8,128)S(1)} %get-tuple-element.236), channel_id=1, source_target_pairs={{8,0},{16,8},{24,16},{32,24},{40,32},{48,40},{56,48},{64,56},{72,6... | collective-permute-start | bytes 36872 | tf_op jit(solution)/shard_map/while/body/eval_jaxpr/ppermute | solution.py:25
  307.1 7.8 %collective-permute-start = (f32[48,64]{1,0:T(8,128)S(1)}, f32[48,64]{1,0:T(8,128)S(1)}, u32[]{:S(2)}, u32[]{:S(2)}) collective-permute-start(f32[48,64]{1,0:T(8,128)S(1)} %get-tuple-element.236), channel_id=1, source_target_pairs={{8,0},{16,8},{24,16},{32,24},{40,32},{48,40},{56,48},{64,56},{72,6... | collective-permute-start | bytes 36872 | tf_op jit(solution)/shard_map/while/body/eval_jaxpr/ppermute | solution.py:25
  315.0 7.8 %collective-permute-start = (f32[48,64]{1,0:T(8,128)S(1)}, f32[48,64]{1,0:T(8,128)S(1)}, u32[]{:S(2)}, u32[]{:S(2)}) collective-permute-start(f32[48,64]{1,0:T(8,128)S(1)} %get-tuple-element.236), channel_id=1, source_target_pairs={{8,0},{16,8},{24,16},{32,24},{40,32},{48,40},{56,48},{64,56},{72,6... | collective-permute-start | bytes 36872 | tf_op jit(solution)/shard_map/while/body/eval_jaxpr/ppermute | solution.py:25
  322.8 7.8 %collective-permute-start = (f32[48,64]{1,0:T(8,128)S(1)}, f32[48,64]{1,0:T(8,128)S(1)}, u32[]{:S(2)}, u32[]{:S(2)}) collective-permute-start(f32[48,64]{1,0:T(8,128)S(1)} %get-tuple-element.236), channel_id=1, source_target_pairs={{8,0},{16,8},{24,16},{32,24},{40,32},{48,40},{56,48},{64,56},{72,6... | collective-permute-start | bytes 36872 | tf_op jit(solution)/shard_map/while/body/eval_jaxpr/ppermute | solution.py:25
  330.7 7.8 %collective-permute-start = (f32[48,64]{1,0:T(8,128)S(1)}, f32[48,64]{1,0:T(8,128)S(1)}, u32[]{:S(2)}, u32[]{:S(2)}) collective-permute-start(f32[48,64]{1,0:T(8,128)S(1)} %get-tuple-element.236), channel_id=1, source_target_pairs={{8,0},{16,8},{24,16},{32,24},{40,32},{48,40},{56,48},{64,56},{72,6... | collective-permute-start | bytes 36872 | tf_op jit(solution)/shard_map/while/body/eval_jaxpr/ppermute | solution.py:25
  338.5 7.8 %collective-permute-start = (f32[48,64]{1,0:T(8,128)S(1)}, f32[48,64]{1,0:T(8,128)S(1)}, u32[]{:S(2)}, u32[]{:S(2)}) collective-permute-start(f32[48,64]{1,0:T(8,128)S(1)} %get-tuple-element.236), channel_id=1, source_target_pairs={{8,0},{16,8},{24,16},{32,24},{40,32},{48,40},{56,48},{64,56},{72,6... | collective-permute-start | bytes 36872 | tf_op jit(solution)/shard_map/while/body/eval_jaxpr/ppermute | solution.py:25
  346.3 7.8 %collective-permute-start = (f32[48,64]{1,0:T(8,128)S(1)}, f32[48,64]{1,0:T(8,128)S(1)}, u32[]{:S(2)}, u32[]{:S(2)}) collective-permute-start(f32[48,64]{1,0:T(8,128)S(1)} %get-tuple-element.236), channel_id=1, source_target_pairs={{8,0},{16,8},{24,16},{32,24},{40,32},{48,40},{56,48},{64,56},{72,6... | collective-permute-start | bytes 36872 | tf_op jit(solution)/shard_map/while/body/eval_jaxpr/ppermute | solution.py:25
  354.2 7.8 %collective-permute-start = (f32[48,64]{1,0:T(8,128)S(1)}, f32[48,64]{1,0:T(8,128)S(1)}, u32[]{:S(2)}, u32[]{:S(2)}) collective-permute-start(f32[48,64]{1,0:T(8,128)S(1)} %get-tuple-element.236), channel_id=1, source_target_pairs={{8,0},{16,8},{24,16},{32,24},{40,32},{48,40},{56,48},{64,56},{72,6... | collective-permute-start | bytes 36872 | tf_op jit(solution)/shard_map/while/body/eval_jaxpr/ppermute | solution.py:25
  362.0 7.8 %collective-permute-start = (f32[48,64]{1,0:T(8,128)S(1)}, f32[48,64]{1,0:T(8,128)S(1)}, u32[]{:S(2)}, u32[]{:S(2)}) collective-permute-start(f32[48,64]{1,0:T(8,128)S(1)} %get-tuple-element.236), channel_id=1, source_target_pairs={{8,0},{16,8},{24,16},{32,24},{40,32},{48,40},{56,48},{64,56},{72,6... | collective-permute-start | bytes 36872 | tf_op jit(solution)/shard_map/while/body/eval_jaxpr/ppermute | solution.py:25
  369.8 7.8 %collective-permute-start = (f32[48,64]{1,0:T(8,128)S(1)}, f32[48,64]{1,0:T(8,128)S(1)}, u32[]{:S(2)}, u32[]{:S(2)}) collective-permute-start(f32[48,64]{1,0:T(8,128)S(1)} %get-tuple-element.236), channel_id=1, source_target_pairs={{8,0},{16,8},{24,16},{32,24},{40,32},{48,40},{56,48},{64,56},{72,6... | collective-permute-start | bytes 36872 | tf_op jit(solution)/shard_map/while/body/eval_jaxpr/ppermute | solution.py:25
  377.7 7.8 %collective-permute-start = (f32[48,64]{1,0:T(8,128)S(1)}, f32[48,64]{1,0:T(8,128)S(1)}, u32[]{:S(2)}, u32[]{:S(2)}) collective-permute-start(f32[48,64]{1,0:T(8,128)S(1)} %get-tuple-element.236), channel_id=1, source_target_pairs={{8,0},{16,8},{24,16},{32,24},{40,32},{48,40},{56,48},{64,56},{72,6... | collective-permute-start | bytes 36872 | tf_op jit(solution)/shard_map/while/body/eval_jaxpr/ppermute | solution.py:25
  385.5 7.8 %collective-permute-start = (f32[48,64]{1,0:T(8,128)S(1)}, f32[48,64]{1,0:T(8,128)S(1)}, u32[]{:S(2)}, u32[]{:S(2)}) collective-permute-start(f32[48,64]{1,0:T(8,128)S(1)} %get-tuple-element.236), channel_id=1, source_target_pairs={{8,0},{16,8},{24,16},{32,24},{40,32},{48,40},{56,48},{64,56},{72,6... | collective-permute-start | bytes 36872 | tf_op jit(solution)/shard_map/while/body/eval_jaxpr/ppermute | solution.py:25
  393.4 7.8 %collective-permute-start = (f32[48,64]{1,0:T(8,128)S(1)}, f32[48,64]{1,0:T(8,128)S(1)}, u32[]{:S(2)}, u32[]{:S(2)}) collective-permute-start(f32[48,64]{1,0:T(8,128)S(1)} %get-tuple-element.236), channel_id=1, source_target_pairs={{8,0},{16,8},{24,16},{32,24},{40,32},{48,40},{56,48},{64,56},{72,6... | collective-permute-start | bytes 36872 | tf_op jit(solution)/shard_map/while/body/eval_jaxpr/ppermute | solution.py:25
  401.2 7.8 %collective-permute-start = (f32[48,64]{1,0:T(8,128)S(1)}, f32[48,64]{1,0:T(8,128)S(1)}, u32[]{:S(2)}, u32[]{:S(2)}) collective-permute-start(f32[48,64]{1,0:T(8,128)S(1)} %get-tuple-element.236), channel_id=1, source_target_pairs={{8,0},{16,8},{24,16},{32,24},{40,32},{48,40},{56,48},{64,56},{72,6... | collective-permute-start | bytes 36872 | tf_op jit(solution)/shard_map/while/body/eval_jaxpr/ppermute | solution.py:25
  409.0 7.8 %collective-permute-start = (f32[48,64]{1,0:T(8,128)S(1)}, f32[48,64]{1,0:T(8,128)S(1)}, u32[]{:S(2)}, u32[]{:S(2)}) collective-permute-start(f32[48,64]{1,0:T(8,128)S(1)} %get-tuple-element.236), channel_id=1, source_target_pairs={{8,0},{16,8},{24,16},{32,24},{40,32},{48,40},{56,48},{64,56},{72,6... | collective-permute-start | bytes 36872 | tf_op jit(solution)/shard_map/while/body/eval_jaxpr/ppermute | solution.py:25
  416.9 7.8 %collective-permute-start = (f32[48,64]{1,0:T(8,128)S(1)}, f32[48,64]{1,0:T(8,128)S(1)}, u32[]{:S(2)}, u32[]{:S(2)}) collective-permute-start(f32[48,64]{1,0:T(8,128)S(1)} %get-tuple-element.236), channel_id=1, source_target_pairs={{8,0},{16,8},{24,16},{32,24},{40,32},{48,40},{56,48},{64,56},{72,6... | collective-permute-start | bytes 36872 | tf_op jit(solution)/shard_map/while/body/eval_jaxpr/ppermute | solution.py:25
  424.7 7.8 %collective-permute-start = (f32[48,64]{1,0:T(8,128)S(1)}, f32[48,64]{1,0:T(8,128)S(1)}, u32[]{:S(2)}, u32[]{:S(2)}) collective-permute-start(f32[48,64]{1,0:T(8,128)S(1)} %get-tuple-element.236), channel_id=1, source_target_pairs={{8,0},{16,8},{24,16},{32,24},{40,32},{48,40},{56,48},{64,56},{72,6... | collective-permute-start | bytes 36872 | tf_op jit(solution)/shard_map/while/body/eval_jaxpr/ppermute | solution.py:25
  432.6 7.8 %collective-permute-start = (f32[48,64]{1,0:T(8,128)S(1)}, f32[48,64]{1,0:T(8,128)S(1)}, u32[]{:S(2)}, u32[]{:S(2)}) collective-permute-start(f32[48,64]{1,0:T(8,128)S(1)} %get-tuple-element.236), channel_id=1, source_target_pairs={{8,0},{16,8},{24,16},{32,24},{40,32},{48,40},{56,48},{64,56},{72,6... | collective-permute-start | bytes 36872 | tf_op jit(solution)/shard_map/while/body/eval_jaxpr/ppermute | solution.py:25
  440.4 7.8 %collective-permute-start = (f32[48,64]{1,0:T(8,128)S(1)}, f32[48,64]{1,0:T(8,128)S(1)}, u32[]{:S(2)}, u32[]{:S(2)}) collective-permute-start(f32[48,64]{1,0:T(8,128)S(1)} %get-tuple-element.236), channel_id=1, source_target_pairs={{8,0},{16,8},{24,16},{32,24},{40,32},{48,40},{56,48},{64,56},{72,6... | collective-permute-start | bytes 36872 | tf_op jit(solution)/shard_map/while/body/eval_jaxpr/ppermute | solution.py:25
  448.2 7.8 %collective-permute-start = (f32[48,64]{1,0:T(8,128)S(1)}, f32[48,64]{1,0:T(8,128)S(1)}, u32[]{:S(2)}, u32[]{:S(2)}) collective-permute-start(f32[48,64]{1,0:T(8,128)S(1)} %get-tuple-element.236), channel_id=1, source_target_pairs={{8,0},{16,8},{24,16},{32,24},{40,32},{48,40},{56,48},{64,56},{72,6... | collective-permute-start | bytes 36872 | tf_op jit(solution)/shard_map/while/body/eval_jaxpr/ppermute | solution.py:25
  456.1 7.8 %collective-permute-start = (f32[48,64]{1,0:T(8,128)S(1)}, f32[48,64]{1,0:T(8,128)S(1)}, u32[]{:S(2)}, u32[]{:S(2)}) collective-permute-start(f32[48,64]{1,0:T(8,128)S(1)} %get-tuple-element.236), channel_id=1, source_target_pairs={{8,0},{16,8},{24,16},{32,24},{40,32},{48,40},{56,48},{64,56},{72,6... | collective-permute-start | bytes 36872 | tf_op jit(solution)/shard_map/while/body/eval_jaxpr/ppermute | solution.py:25
  463.9 7.8 %collective-permute-start = (f32[48,64]{1,0:T(8,128)S(1)}, f32[48,64]{1,0:T(8,128)S(1)}, u32[]{:S(2)}, u32[]{:S(2)}) collective-permute-start(f32[48,64]{1,0:T(8,128)S(1)} %get-tuple-element.236), channel_id=1, source_target_pairs={{8,0},{16,8},{24,16},{32,24},{40,32},{48,40},{56,48},{64,56},{72,6... | collective-permute-start | bytes 36872 | tf_op jit(solution)/shard_map/while/body/eval_jaxpr/ppermute | solution.py:25
  471.7 7.8 %collective-permute-start = (f32[48,64]{1,0:T(8,128)S(1)}, f32[48,64]{1,0:T(8,128)S(1)}, u32[]{:S(2)}, u32[]{:S(2)}) collective-permute-start(f32[48,64]{1,0:T(8,128)S(1)} %get-tuple-element.236), channel_id=1, source_target_pairs={{8,0},{16,8},{24,16},{32,24},{40,32},{48,40},{56,48},{64,56},{72,6... | collective-permute-start | bytes 36872 | tf_op jit(solution)/shard_map/while/body/eval_jaxpr/ppermute | solution.py:25
  479.6 7.8 %collective-permute-start = (f32[48,64]{1,0:T(8,128)S(1)}, f32[48,64]{1,0:T(8,128)S(1)}, u32[]{:S(2)}, u32[]{:S(2)}) collective-permute-start(f32[48,64]{1,0:T(8,128)S(1)} %get-tuple-element.236), channel_id=1, source_target_pairs={{8,0},{16,8},{24,16},{32,24},{40,32},{48,40},{56,48},{64,56},{72,6... | collective-permute-start | bytes 36872 | tf_op jit(solution)/shard_map/while/body/eval_jaxpr/ppermute | solution.py:25
  487.4 7.8 %collective-permute-start = (f32[48,64]{1,0:T(8,128)S(1)}, f32[48,64]{1,0:T(8,128)S(1)}, u32[]{:S(2)}, u32[]{:S(2)}) collective-permute-start(f32[48,64]{1,0:T(8,128)S(1)} %get-tuple-element.236), channel_id=1, source_target_pairs={{8,0},{16,8},{24,16},{32,24},{40,32},{48,40},{56,48},{64,56},{72,6... | collective-permute-start | bytes 36872 | tf_op jit(solution)/shard_map/while/body/eval_jaxpr/ppermute | solution.py:25
  495.3 7.8 %collective-permute-start = (f32[48,64]{1,0:T(8,128)S(1)}, f32[48,64]{1,0:T(8,128)S(1)}, u32[]{:S(2)}, u32[]{:S(2)}) collective-permute-start(f32[48,64]{1,0:T(8,128)S(1)} %get-tuple-element.236), channel_id=1, source_target_pairs={{8,0},{16,8},{24,16},{32,24},{40,32},{48,40},{56,48},{64,56},{72,6... | collective-permute-start | bytes 36872 | tf_op jit(solution)/shard_map/while/body/eval_jaxpr/ppermute | solution.py:25
  503.1 7.8 %collective-permute-start = (f32[48,64]{1,0:T(8,128)S(1)}, f32[48,64]{1,0:T(8,128)S(1)}, u32[]{:S(2)}, u32[]{:S(2)}) collective-permute-start(f32[48,64]{1,0:T(8,128)S(1)} %get-tuple-element.236), channel_id=1, source_target_pairs={{8,0},{16,8},{24,16},{32,24},{40,32},{48,40},{56,48},{64,56},{72,6... | collective-permute-start | bytes 36872 | tf_op jit(solution)/shard_map/while/body/eval_jaxpr/ppermute | solution.py:25
  510.9 7.8 %collective-permute-start = (f32[48,64]{1,0:T(8,128)S(1)}, f32[48,64]{1,0:T(8,128)S(1)}, u32[]{:S(2)}, u32[]{:S(2)}) collective-permute-start(f32[48,64]{1,0:T(8,128)S(1)} %get-tuple-element.236), channel_id=1, source_target_pairs={{8,0},{16,8},{24,16},{32,24},{40,32},{48,40},{56,48},{64,56},{72,6... | collective-permute-start | bytes 36872 | tf_op jit(solution)/shard_map/while/body/eval_jaxpr/ppermute | solution.py:25
  518.8 0.6 copy-start.2
Sparse Core Ops, SparseCore 0:
  9.2 64.8 all-gather.3
  75.9 62.5 all-gather.5
  155.3 77.8 reduce-scatter.1
where the time goes:
time: 527 us; the launch traced here: 526 us
  waiting for transfers between devices  383 us (73%)
  starting transfers between devices  59.4 us (11%)
  blocking collectives  40.8 us (8%)
  matrix products  19.7 us (4%)
  between operations  15.1 us (3%)
  other arithmetic  6.45 us (1%)
    ppermute x31, waiting for transfers between devices, from_behind(): lax.ppermute(value, axis, [(source, source + steps) for source in range(l...  183 us
    reduce_scatter x1, waiting for transfers between devices, body(): drift = lax.psum_scatter(term, 'tensor', scatter_dimension=0, tiled=True)  76.7 us
    all_gather x1, waiting for transfers between devices, body(): lax.all_gather(w_down, 'tm', axis=1, tiled=True)  64.4 us
    ppermute x31, starting transfers between devices, from_behind(): lax.ppermute(value, axis, [(source, source + steps) for source in range(l...  59.3 us
    all_gather x1, waiting for transfers between devices, body(): lax.all_gather(w_up, 'tm', axis=0, tiled=True)  57.6 us
    all_gather x1, blocking collectives, carried_in(): gathered = lax.all_gather(part, axis)  40.8 us
    dot_general x1, matrix products, body(): jnp.dot(active, lax.all_gather(w_down, 'tm', axis=1, tiled=True), preferr...  11.1 us
  transfers between devices with their start and end apart: 34, of which 34 were waited for; matrix products, arithmetic and copies ran while one was open for 1% of the time, Pallas kernels for 0%

commit v1 on v0

v1 whole, which is shorter than its diff:
```python
import functools
import math

import jax
import jax.numpy as jnp
import numpy as np
from jax import lax
from jax.experimental import pallas as pl
from jax.experimental.pallas import tpu as pltpu
from jax.sharding import PartitionSpec as P

SCHED = 1000
D, FFB, LAT, TEMB, TOK = 3072, 768, 64, 256, 384
HALF = FFB // 2
ROWS = 192
F32, BF16 = jnp.float32, jnp.bfloat16
NT = (((1,), (1,)), ((), ()))


def nt_dot(a, b):
    return lax.dot_general(a, b, NT, preferred_element_type=F32)


def dot(a, b):
    return jnp.dot(a, b, preferred_element_type=F32)


def eye(n):
    i = lax.broadcasted_iota(jnp.int32, (n, n), 0)
    j = lax.broadcasted_iota(jnp.int32, (n, n), 1)
    return jnp.where(i == j, 1.0, 0.0).astype(BF16)


def device(x, zl, c, y, zh):
    return (x * 8 + zl * 2 + c, y * 2 + zh)


def kernel(
    hid_h, base_v, wmod_h, wup_h, wdn_h, wout_h, freq_v, times_s, sched_s, slide_s,
    out_v,
    hid, wmod, wdn, wout, normed, wup, wdg, wdstage, ctile, mods, gch, gbuf, psend, pown, pin,
    w2t, pre, act, head, part, prt, qy, ry, rz, zin, xsend, xin,
    loc, up_s, up_r, dn_s, dn_r, nm_s, nm_r, ct_s, ct_r, zs_own, zs_fwd, zr, xs, xf, xr, xo,
    ps_s, ps_r, pt_s, pt_r, ya_s, ya_r, za_s, za_r, xa_s, xa_r,
):
    tm, te = lax.axis_index("tm"), lax.axis_index("tensor")
    x, zl, c = tm // 8, (tm // 2) % 4, tm % 2
    y, zh = te // 2, te % 2
    place = x * 4 + zl
    partner = device(x, zl, 1 - c, y, zh)
    z = zh * 4 + zl

    def at_x(d, core=c):
        return device((x + d) % 4, zl, core, y, zh)

    def at_zl(zp, core=c):
        return device(x, zp, core, y, zh)

    def at_z(d):
        zp = (z + d) % 8
        return device(x, zp % 4, c, y, zp // 4)

    def at_y(d):
        return device(x, zl, c, (y + d) % 4, zh)

    def send(src, dst, ssem, rsem, dev):
        return pltpu.make_async_remote_copy(
            src_ref=src, dst_ref=dst, send_sem=ssem, recv_sem=rsem,
            device_id=dev, device_id_type=pl.DeviceIdType.MESH,
        )

    barrier = pltpu.get_barrier_semaphore()

    def greet(dev):
        pl.semaphore_signal(barrier, inc=1, device_id=dev, device_id_type=pl.DeviceIdType.MESH)

    greet(partner)
    for d in (1, 2, 3):
        greet(at_x(d))
        greet(at_x(d, 1 - c))
        greet(at_y(d))
        greet(at_zl((zl + d) % 4, 1 - c))
    for d in range(1, 8):
        greet(at_z(d))

    my_rows = pl.ds(pl.multiple_of(place * ROWS + c * 96, 32), 96)
    mine = pl.ds(pl.multiple_of(c * HALF, 128), HALF)
    other = pl.ds(pl.multiple_of((1 - c) * HALF, 128), HALF)
    cp_up = pltpu.make_async_copy(wup_h.at[:, mine], wup.at[my_rows, :], loc.at[0])
    cp_dn = pltpu.make_async_copy(wdn_h, wdn, loc.at[1])
    cp_ss = pltpu.make_async_copy(wmod_h.at[:, : 2 * D], wmod.at[:, : 2 * D], loc.at[2])
    cp_hid = pltpu.make_async_copy(hid_h, hid, loc.at[3])
    cp_gate = pltpu.make_async_copy(wmod_h.at[:, 2 * D :], wmod.at[:, 2 * D :], loc.at[4])
    cp_out = pltpu.make_async_copy(wout_h, wout, loc.at[5])
    for cp in (cp_up, cp_dn, cp_ss, cp_hid, cp_gate, cp_out):
        cp.start()

    t = times_s[0].astype(F32)
    angles = freq_v[...] * t
    emb = jnp.concatenate([jnp.cos(angles), jnp.sin(angles)], axis=1)
    cond = (emb * jax.nn.sigmoid(emb)).astype(BF16).astype(F32)
    step = 0.1 + 0.3 * sched_s[0].astype(F32) / SCHED
    slot = zl * 2 + c
    tile = jnp.concatenate([cond, jnp.full((8, 128), 1.0, F32) * step], axis=1)
    rowid = lax.broadcasted_iota(jnp.int32, (8, TEMB + 128), 0)
    ctile[slot] = jnp.where(rowid == slot, tile, 0.0)
    cond_b = cond.astype(BF16)

    pl.semaphore_wait(barrier, 20)

    up_x = send(wup_h.at[:, other], wup.at[my_rows, :], up_s, up_r, partner)
    up_x.start()
    ct = []
    for d in range(1, 8):
        to = (slot + d) % 8
        ct.append(send(ctile.at[slot], ctile.at[slot], ct_s.at[d], ct_r.at[d], at_zl(to // 2, to % 2)))
        ct[-1].start()

    cp_dn.wait()
    own_half = pl.ds(pl.multiple_of(c * 96, 32), 96)
    wdstage[0] = nt_dot(eye(96), wdn[:HALF, :]).astype(BF16)
    wdstage[1] = nt_dot(eye(96), wdn[HALF:, :]).astype(BF16)
    dn_x = send(wdstage.at[1 - c], wdg.at[x, own_half, :], dn_s, dn_r, partner)
    dn_x.start()
    wdg[x, own_half, :] = wdstage[c]

    m = zl // 2
    zz = zl + m * (3 - 2 * zl)
    order = [k + m * (3 - 2 * k) for k in (zz, 1 - zz, 2, 3)]

    def rows_of(xp, zp, lo=0, n=ROWS):
        return pl.ds(pl.multiple_of((xp * 4 + zp) * ROWS + lo, 32), n)

    def block(xp, k, lo=0, n=ROWS):
        if k == 4:
            return wdg.at[xp, pl.ds(lo, n), :]
        return wup.at[rows_of(xp, order[k], lo, n), :]

    left, right, far = (x + 3) % 4, (x + 1) % 4, (x + 2) % 4

    def x_out(k):
        return [
            send(block(x, k), block(x, k), xs.at[k, 0], xr.at[k, 0], at_x(1)),
            send(block(x, k), block(x, k), xs.at[k, 1], xr.at[k, 1], at_x(3)),
        ]

    def x_fwd(k):
        return [
            send(block(left, k, 0, 96), block(left, k, 0, 96), xf.at[k, 0], xo.at[k, 0], at_x(1)),
            send(block(right, k, 96, 96), block(right, k, 96, 96), xf.at[k, 1], xo.at[k, 1], at_x(3)),
        ]

    def x_start(k):
        for cp in x_out(k):
            cp.start()

    def x_relay(k):
        send(block(left, k), block(left, k), xs.at[k, 0], xr.at[k, 0], at_x(1)).wait_recv()
        fw = x_fwd(k)
        fw[0].start()
        send(block(right, k), block(right, k), xs.at[k, 1], xr.at[k, 1], at_x(3)).wait_recv()
        fw[1].start()

    def x_last(k):
        send(block(far, k, 0, 96), block(far, k, 0, 96), xf.at[k, 0], xo.at[k, 0], at_x(1)).wait_recv()
        send(block(far, k, 96, 96), block(far, k, 96, 96), xf.at[k, 1], xo.at[k, 1], at_x(3)).wait_recv()

    def z_send(k, ssem, to):
        return send(block(x, k), block(x, k), ssem, zr.at[order[k]], at_zl(to))

    def z_fwd(k, act_on):
        zp = order[k]

        @pl.when(jnp.logical_and(zp < zl, zl < 3))
        def _():
            act_on(z_send(k, zs_fwd.at[k], zl + 1))

        @pl.when(jnp.logical_and(zp > zl, zl > 0))
        def _():
            act_on(z_send(k, zs_fwd.at[k], zl - 1))

    def z_relay(k):
        z_send(k, zs_fwd.at[k], zl).wait_recv()
        z_fwd(k, lambda cp: cp.start())

    def z_own(act_on):
        @pl.when(zl < 3)
        def _():
            act_on(z_send(0, zs_own.at[0], zl + 1))

        @pl.when(zl > 0)
        def _():
            act_on(z_send(0, zs_own.at[1], zl - 1))

    cp_up.wait()
    up_x.wait_recv()
    x_start(0)
    z_own(lambda cp: cp.start())
    dn_x.wait_recv()
    x_start(4)

    cp_ss.wait()

    def mod_cols(i, _):
        cols = pl.ds(pl.multiple_of(i * 512, 512), 512)
        mods[:, cols] = dot(cond_b, wmod[:, cols])
        return 0

    lax.fori_loop(0, 12, mod_cols, 0)
    cp_hid.wait()

    def norm_rows(i, _):
        rows = pl.ds(pl.multiple_of(i * 16, 16), 16)
        v = hid[rows, :].astype(F32)
        mean = jnp.sum(v, axis=1, keepdims=True) * (1.0 / D)
        v = v - mean
        var = jnp.sum(v * v, axis=1, keepdims=True) * (1.0 / D)
        v = v * lax.rsqrt(var + 1e-06)
        v = v * (1.0 + mods[0:1, D:]) + mods[0:1, :D]
        normed[pl.ds(pl.multiple_of(c * TOK + i * 16, 16), 16), :] = v.astype(BF16)
        return 0

    def norm_copy(q):
        rows = pl.ds(pl.multiple_of(c * TOK + q * 96, 32), 96)
        return send(normed.at[rows, :], normed.at[rows, :], nm_s.at[q], nm_r.at[q], partner)

    for q in range(2):
        lax.fori_loop(q * 6, q * 6 + 6, norm_rows, 0)
        norm_copy(q).start()

    z_relay(1)
    x_relay(0)
    x_start(1)
    for q in range(2, 4):
        lax.fori_loop(q * 6, q * 6 + 6, norm_rows, 0)
        norm_copy(q).start()
    x_relay(4)

    cp_out.wait()
    share = pl.ds(pl.multiple_of(te * 384, 128), 384)
    wo = wout[share, :].astype(F32)
    wo = jnp.concatenate([wo, wo], axis=1)
    lane = lax.broadcasted_iota(jnp.int32, (384, 128), 1)
    wo = jnp.where(lane // 64 == c, wo, 0.0).astype(BF16)
    head[...] = dot(hid[:, share], wo)

    for d in range(1, 8):
        frm = (slot + 8 - d) % 8
        send(ctile.at[frm], ctile.at[frm], ct_s.at[d], ct_r.at[d], partner).wait_recv()
    cp_gate.wait()
    cond8 = ctile[0, :, :TEMB]
    for s in range(1, 8):
        cond8 = cond8 + ctile[s, :, :TEMB]
    cond8 = cond8.astype(BF16)
    for i in range(8):
        g = dot(cond8, wmod[:, 2 * D + i * 384 : 2 * D + (i + 1) * 384])
        gch[2 * i] = g[:, :ROWS]
        gch[2 * i + 1] = g[:, ROWS:]
    eye64 = eye(64)

    def gate_head(xp, _):
        p = xp * 4 + zl
        wt = nt_dot(eye64, wout[pl.ds(pl.multiple_of(p * ROWS, 32), ROWS), :])
        for s in range(8):
            g = gch[p, s : s + 1, :] * wt
            hi = g.astype(BF16)
            gbuf[xp, s * 64 : (s + 1) * 64, :] = hi
            gbuf[xp, 512 + s * 64 : 512 + (s + 1) * 64, :] = (g - hi.astype(F32)).astype(BF16)
        return 0

    lax.fori_loop(0, 4, gate_head, 0)

    z_relay(2)
    x_relay(1)
    x_start(2)

    x_last(4)

    def partial(zp, _):
        hi_rows = pl.ds(pl.multiple_of(zp * 128, 128), 128)
        lo_rows = pl.ds(pl.multiple_of(512 + zp * 128, 128), 128)
        acc = jnp.zeros((128, HALF), F32)
        for xp in range(4):
            acc = acc + dot(gbuf[xp, hi_rows, :], wdg[xp]) + dot(gbuf[xp, lo_rows, :], wdg[xp])
        psend[zp] = acc.astype(BF16)

        @pl.when(zp == zl)
        def _():
            pown[...] = acc

        return 0

    lax.fori_loop(0, 4, partial, 0)
    pcopies = []
    for d in (1, 2, 3):
        to = (zl + d) % 4
        pcopies.append(send(psend.at[to], pin.at[zl], ps_s.at[d - 1], ps_r.at[d - 1], at_zl(to)))
        pcopies[-1].start()

    for q in range(4):
        norm_rows_in = pl.ds(pl.multiple_of((1 - c) * TOK + q * 96, 32), 96)
        send(normed.at[norm_rows_in, :], normed.at[norm_rows_in, :], nm_s.at[q], nm_r.at[q], partner).wait_recv()
    x_last(0)
    z_relay(3)
    x_relay(2)
    x_start(3)
    x_last(1)

    def chunk(xp, mm):
        return pl.ds(pl.multiple_of((xp * 2 + mm) * 384, 128), 384)

    def up(xps, mm, first):
        def tile_rows(i, _):
            rows = pl.ds(pl.multiple_of(i * 128, 128), 128)
            acc = None if first else pre[rows, :]
            for xp in xps:
                v = dot(normed[rows, chunk(xp, mm)], wup[chunk(xp, mm), :])
                acc = v if acc is None else acc + v
            pre[rows, :] = acc
            return 0

        lax.fori_loop(0, 6, tile_rows, 0)

    up([x, left, right, far], m, True)
    x_relay(3)
    up([x, left, right], 1 - m, False)

    w2 = pown[...]
    for d in (1, 2, 3):
        frm = (zl + 4 - d) % 4
        send(psend.at[frm], pin.at[frm], ps_s.at[d - 1], ps_r.at[d - 1], at_zl(frm)).wait_recv()
        w2 = w2 + pin[frm].astype(F32)
    hi = w2.astype(BF16)
    lo = (w2 - hi.astype(F32)).astype(BF16)
    w2t[...] = jnp.zeros((256, 768), BF16)
    w2t[0:64, 0:384] = hi[:64]
    w2t[64:128, 384:768] = hi[64:]
    w2t[128:192, 0:384] = lo[:64]
    w2t[192:256, 384:768] = lo[64:]

    lane1 = lax.broadcasted_iota(jnp.int32, (1, 128), 1)
    step0 = jnp.sum(ctile[zl * 2, :, TEMB:], axis=0, keepdims=True)
    step1 = jnp.sum(ctile[zl * 2 + 1, :, TEMB:], axis=0, keepdims=True)
    steps = jnp.where(lane1 < 64, step0, step1)

    x_last(2)
    x_last(3)

    def finish(i, _):
        rows = pl.ds(pl.multiple_of(i * 128, 128), 128)
        for j in range(2):
            jr = pl.ds(pl.multiple_of(j * TOK + i * 128, 128), 128)
            v = pre[jr, :] + dot(normed[jr, chunk(far, 1 - m)], wup[chunk(far, 1 - m), :])
            act[:, j * HALF : (j + 1) * HALF] = jax.nn.gelu(v, approximate=True).astype(BF16)
        r = nt_dot(act[...], w2t[...])
        part[rows, :] = (r[:, :128] + r[:, 128:] + head[rows, :] * 1.0) * steps
        return 0

    lax.fori_loop(0, 3, finish, 0)

    pt = []
    for b in range(8):
        rows = pl.ds(pl.multiple_of(b * 48 + (1 - c) * 24, 8), 24)
        pt.append(send(part.at[rows, :], prt.at[b], pt_s.at[b], pt_r.at[b], partner))
        pt[-1].start()
    for b in range(8):
        pt[b].wait_recv()
        qy[b] = part[pl.ds(pl.multiple_of(b * 48 + c * 24, 8), 24), :] + prt[b]
    ya = []
    for d in (1, 2, 3):
        to = (y + d) % 4
        ya.append(send(qy.at[pl.ds(to * 2, 2)], ry.at[d - 1], ya_s.at[d - 1], ya_r.at[d - 1], at_y(d)))
        ya[-1].start()
    tot = qy[pl.ds(y * 2, 2)]
    for d in (1, 2, 3):
        ya[d - 1].wait_recv()
        tot = tot + ry[d - 1]
    rz[...] = tot
    za = []
    for d in range(1, 8):
        to = (z + d) % 8
        za.append(send(rz.at[to // 4], zin.at[z], za_s.at[d - 1], za_r.at[d - 1], at_z(d)))
        za[-1].start()
    zin[z] = rz[zh]
    for d in range(1, 8):
        frm = (z + 8 - d) % 8
        send(rz.at[0], zin.at[frm], za_s.at[d - 1], za_r.at[d - 1], at_z(d)).wait_recv()
    vs = [zin[i] + zin[4 + i] for i in range(4)]
    slide = slide_s[0]
    lane24 = lax.broadcasted_iota(jnp.int32, (24, 128), 1) // 64
    xa = []

    def prefix(xp, cp):
        last = xp * 8 + zl * 2 + cp + slide - 1
        acc = jnp.zeros((24, 128), F32)
        for i in range(4):
            acc = acc + jnp.where(lane24 + (x * 8 + i * 2) <= last, vs[i], 0.0)
        return acc + pltpu.roll(acc, 64, 1)

    for d in range(4):
        for e in range(2):
            if d == 0 and e == 0:
                continue
            n = d * 2 + e
            core = (c + e) % 2
            xsend[n] = prefix((x + d) % 4, core)
            xa.append((send(xsend.at[n], xin.at[x, c], xa_s.at[n], xa_r.at[n], at_x(d, core)), d, e))
            xa[-1][0].start()
    xin[x, c] = prefix(x, c)
    for cp, d, e in xa:
        send(xsend.at[d * 2 + e], xin.at[(x + 4 - d) % 4, (c + e) % 2], xa_s.at[d * 2 + e], xa_r.at[d * 2 + e], partner).wait_recv()
    for h in range(2):
        s = xin[0, h] + xin[1, h] + xin[2, h] + xin[3, h]
        out_v[h * 24 : (h + 1) * 24, :] = base_v[h * 24 : (h + 1) * 24, :] + s[:, :64]

    up_x.wait_send()
    dn_x.wait_send()
    for cp in ct + pcopies + pt + ya + za:
        cp.wait_send()
    for cp, _, _ in xa:
        cp.wait_send()
    for q in range(4):
        norm_copy(q).wait_send()
    for k in range(5):
        for cp in x_out(k) + x_fwd(k):
            cp.wait_send()
    z_own(lambda cp: cp.wait_send())
    for k in (1, 2, 3):
        z_fwd(k, lambda cp: cp.wait_send())


def body(hidden_state, base_latent, w_modulation, w_up, w_down, w_out, times, sched_index, slide_count):
    half = TEMB // 2
    freqs = np.exp(-math.log(10000.0) * np.arange(half, dtype=np.float32) / half).astype(np.float32)
    freqs = jnp.asarray(np.broadcast_to(freqs, (8, half)))
    any_, vmem, smem = (pl.BlockSpec(memory_space=s) for s in (pl.ANY, pltpu.VMEM, pltpu.SMEM))
    V, dma = pltpu.VMEM, pltpu.SemaphoreType.DMA
    out = pl.pallas_call(
        kernel,
        out_shape=jax.ShapeDtypeStruct((48, LAT), F32),
        in_specs=[any_, vmem, any_, any_, any_, any_, vmem, smem, smem, smem],
        out_specs=vmem,
        scratch_shapes=[
            V((TOK, D), BF16),
            V((TEMB, 3 * D), BF16),
            V((FFB, 96), BF16),
            V((D, LAT), BF16),
            V((2 * TOK, D), BF16),
            V((D, HALF), BF16),
            V((4, ROWS, HALF), BF16),
            V((2, 96, HALF), BF16),
            V((8, 8, TEMB + 128), F32),
            V((8, 2 * D), F32),
            V((16, 8, ROWS), F32),
            V((4, 1024, ROWS), BF16),
            V((4, 128, HALF), BF16),
            V((128, HALF), F32),
            V((4, 128, HALF), BF16),
            V((256, 768), BF16),
            V((2 * TOK, HALF), F32),
            V((128, 2 * HALF), BF16),
            V((TOK, 128), F32),
            V((TOK, 128), F32),
            V((8, 24, 128), F32),
            V((8, 24, 128), F32),
            V((3, 2, 24, 128), F32),
            V((2, 24, 128), F32),
            V((8, 24, 128), F32),
            V((8, 24, 128), F32),
            V((4, 2, 24, 128), F32),
            dma((6,)),
            dma, dma, dma, dma,
            dma((4,)), dma((4,)),
            dma((8,)), dma((8,)),
            dma((2,)), dma((4,)), dma((4,)),
            dma((5, 2)), dma((5, 2)), dma((5, 2)), dma((5, 2)),
            dma((3,)), dma((3,)),
            dma((8,)), dma((8,)),
            dma((3,)), dma((3,)),
            dma((7,)), dma((7,)),
            dma((8,)), dma((8,)),
        ],
        compiler_params=pltpu.CompilerParams(
            collective_id=0, has_side_effects=True, vmem_limit_bytes=48 * 2**20
        ),
        cost_estimate=pl.CostEstimate(flops=4 * 10**9, bytes_accessed=10**7, transcendentals=300000),
        name="picard",
    )(
        hidden_state[0], base_latent, w_modulation, w_up, w_down, w_out, freqs,
        times, sched_index, slide_count,
    )
    return out[None]


def solution(mesh):
    placed = (
        P("tm", None, None),
        P("tensor", None),
        P(),
        P("tm", "tensor"),
        P("tensor", "tm"),
        P(),
        P("tm"),
        P("tm"),
        P(),
    )
    return jax.shard_map(
        body, mesh=mesh, in_specs=placed, out_specs=P("tm", "tensor", None), check_vma=False
    )
```

time: 527 us -> 75.2 us (0.14)
  the two profiles are of different devices: /device:TPU:97 before, /device:TPU:1 now
where the time goes in v1:
time: 75.2 us; the launch traced here: 74.9 us
  Pallas kernels  65.9 us (88%)
  local copies, waits for them, and re-layouts  7.03 us (9%)
  between operations  1.97 us (3%)
    pallas_call x1, Pallas kernels, body(): pl.pallas_call(kernel, out_shape=jax.ShapeDtypeStruct((48, LAT), F32), in...  65.9 us
    unnamed x9, local copies, waits for them, and re-layouts  6.37 us

profile of v1, /device:TPU:1, one launch (start us, length us, event | category | flops | bytes accessed | tf_op | source)
XLA Modules:
  0.0 74.9 jit_solution(10552560973337581390)
XLA Ops:
  1.9 1.1 %copy.11.wdn_h = bf16[768,96]{1,0:T(8,128)(2,1)S(1)} copy(bf16[768,96]{0,1:T(8,128)(2,1)} %param.14) | data formatting | bytes 294912 | tf_op args[4]
  3.0 1.4 %copy.12.wout_h = bf16[3072,64]{1,0:T(8,128)(2,1)S(1)} copy(bf16[3072,64]{0,1:T(8,128)(2,1)} %param.15) | data formatting | bytes 786432 | tf_op args[5]
  4.4 0.7 jit_solution_.3.freq_v
  5.1 0.0 copy-start
  5.1 1.7 %copy-done = bf16[1,384,3072]{2,1,0:T(8,128)(2,1)S(1)} copy-done((bf16[1,384,3072]{2,1,0:T(8,128)(2,1)S(1)}, bf16[1,384,3072]{2,1,0:T(8,128)(2,1)}, u32[]{:S(2)}) %copy-start) | copy-done | bytes 2359320
  6.7 0.0 copy-start.1
  6.7 0.9 %copy-done.1 = bf16[96,768]{1,0:T(8,128)(2,1)S(1)} copy-done((bf16[96,768]{1,0:T(8,128)(2,1)S(1)}, bf16[96,768]{1,0:T(8,128)(2,1)}, u32[]{:S(2)}) %copy-start.1) | copy-done | bytes 147480
  7.6 0.0 copy-start.2
  7.6 0.7 copy-done.2
  8.4 65.9 %picard.1 = f32[48,64]{1,0:T(8,128)S(1)} custom-call(bf16[384,3072]{1,0:T(8,128)(2,1)S(1)} %bitcast.3, f32[48,64]{1,0:T(8,128)S(1)} %copy-done.2, bf16[256,9216]{1,0:T(8,128)(2,1)} %wmod_h.1, bf16[96,768]{1,0:T(8,128)(2,1)S(1)} %copy-done.1, bf16[768,96]{1,0:T(8,128)(2,1)S(1)} %copy.11.wdn_h, bf16[3072,64]{1,0:T(8,128)(2,1)S(1)} %copy.12.wout_h, ...), custom_call_target="tpu_custom_call" | custom-call | flops 4000000000 | bytes 10000000 | tf_op jit(solution)/shard_map/picard/pallas_call | solution.py:438
  74.3 0.6 copy.17
Async XLA Ops:
  5.1 1.7 %copy-start = (bf16[1,384,3072]{2,1,0:T(8,128)(2,1)S(1)}, bf16[1,384,3072]{2,1,0:T(8,128)(2,1)}, u32[]{:S(2)}) copy-start(bf16[1,384,3072]{2,1,0:T(8,128)(2,1)} %param.10) | copy-start | bytes 7077892
  6.7 0.9 %copy-start.1 = (bf16[96,768]{1,0:T(8,128)(2,1)S(1)}, bf16[96,768]{1,0:T(8,128)(2,1)}, u32[]{:S(2)}) copy-start(bf16[96,768]{1,0:T(8,128)(2,1)} %wup_h.1) | copy-start | bytes 442372
  7.6 0.7 copy-start.2

commit v2 on v1

v2 whole, which is shorter than its diff:
```python
import functools
import math

import jax
import jax.numpy as jnp
from jax import lax
from jax.experimental import pallas as pl
from jax.experimental.pallas import tpu as pltpu
from jax.sharding import PartitionSpec as P

SCHED = 1000
D, FFB, LAT, TEMB, TOK = 3072, 768, 64, 256, 384
HALF = FFB // 2
ROWS = 192
F32, BF16 = jnp.float32, jnp.bfloat16
NT = (((1,), (1,)), ((), ()))


def nt_dot(a, b):
    return lax.dot_general(a, b, NT, preferred_element_type=F32)


def dot(a, b):
    return jnp.dot(a, b, preferred_element_type=F32)


def device(x, zl, c, y, zh):
    return (x * 8 + zl * 2 + c, y * 2 + zh)


def kernel(
    hid_h, base_h, wmod_h, wup_h, wdn_h, wout_h, times_h, sched_h, slide_h,
    out_v,
    times_s, sched_s, slide_s, hid, wmod, base, wout, normed, wup, wdg, ctile, mods, gch, wch, gbuf, psend, pown, pin,
    w2t, pre, act, head, part, ry, rz, zin, xsend, xin,
    loc, up_s, up_r, dn_s, dn_r, nm_s, nm_r, ct_s, ct_r, zs_own, zs_fwd, zr, xs, xf, xr, xo,
    ps_s, ps_r, ya_s, ya_r, za_s, za_r, xa_s, xa_r,
):
    tm, te = lax.axis_index("tm"), lax.axis_index("tensor")
    x, zl, c = tm // 8, (tm // 2) % 4, tm % 2
    y, zh = te // 2, te % 2
    place = x * 4 + zl
    partner = device(x, zl, 1 - c, y, zh)
    z = zh * 4 + zl

    def at_x(d, core=c):
        return device((x + d) % 4, zl, core, y, zh)

    def at_zl(zp, core=c):
        return device(x, zp, core, y, zh)

    def at_z(d):
        zp = (z + d) % 8
        return device(x, zp % 4, c, y, zp // 4)

    def at_y(d, core=c):
        return device(x, zl, core, (y + d) % 4, zh)

    def send(src, dst, ssem, rsem, dev):
        return pltpu.make_async_remote_copy(
            src_ref=src, dst_ref=dst, send_sem=ssem, recv_sem=rsem,
            device_id=dev, device_id_type=pl.DeviceIdType.MESH,
        )

    barrier = pltpu.get_barrier_semaphore()

    def greet(dev):
        pl.semaphore_signal(barrier, inc=1, device_id=dev, device_id_type=pl.DeviceIdType.MESH)

    greet(partner)
    for d in (1, 2, 3):
        greet(at_x(d))
        greet(at_x(d, 1 - c))
        greet(at_y(d))
        greet(at_y(d, 1 - c))
        greet(at_zl((zl + d) % 4, 1 - c))
    for d in range(1, 8):
        greet(at_z(d))

    my_rows = pl.ds(pl.multiple_of(place * ROWS + c * 96, 32), 96)
    mine = pl.ds(pl.multiple_of(c * HALF, 128), HALF)
    cp_up = pltpu.make_async_copy(wup_h.at[:, mine], wup.at[my_rows, :], loc.at[0])
    own_half = pl.ds(pl.multiple_of(c * 96, 32), 96)
    cp_dn = pltpu.make_async_copy(wdn_h.at[:, mine], wdg.at[x, own_half, :], loc.at[1])
    cp_ss = pltpu.make_async_copy(wmod_h.at[:, : 2 * D], wmod.at[:, : 2 * D], loc.at[2])
    cp_hid = pltpu.make_async_copy(hid_h, hid, loc.at[3])
    cp_gate = pltpu.make_async_copy(wmod_h.at[:, 2 * D :], wmod.at[:, 2 * D :], loc.at[4])
    cp_out = pltpu.make_async_copy(wout_h, wout, loc.at[5])
    cp_base = pltpu.make_async_copy(base_h, base, loc.at[6])
    scalars = [
        pltpu.make_async_copy(a, b, loc.at[7 + i])
        for i, (a, b) in enumerate(((times_h, times_s), (sched_h, sched_s), (slide_h, slide_s)))
    ]
    for cp in scalars:
        cp.start()
    for cp in (cp_up, cp_dn, cp_ss, cp_hid, cp_gate, cp_out, cp_base):
        cp.start()

    for cp in scalars:
        cp.wait()
    t = times_s[0].astype(F32)
    k = lax.broadcasted_iota(jnp.int32, (8, 128), 1).astype(F32)
    angles = jnp.exp(k * (-math.log(10000.0) / 128)) * t
    emb = jnp.concatenate([jnp.cos(angles), jnp.sin(angles)], axis=1)
    cond = (emb * jax.nn.sigmoid(emb)).astype(BF16).astype(F32)
    step = 0.1 + 0.3 * sched_s[0].astype(F32) / SCHED
    slot = zl * 2 + c
    tile = jnp.concatenate([cond, jnp.full((8, 128), 1.0, F32) * step], axis=1)
    rowid = lax.broadcasted_iota(jnp.int32, (8, TEMB + 128), 0)
    ctile[slot] = jnp.where(rowid == slot, tile, 0.0)
    cond_b = cond.astype(BF16)

    pl.semaphore_wait(barrier, 23)

    def own_rows(k, core):
        cols = pl.ds(pl.multiple_of(core * HALF, 128), HALF)
        if k == 4:
            return wdn_h.at[:, cols], wdg.at[x, own_half, :]
        return wup_h.at[:, cols], wup.at[my_rows, :]

    def own_x(k):
        cps = []
        for side in range(2):
            for e in range(2):
                core = (c + e) % 2
                src, dst = own_rows(k, core)
                to = at_x(1 if side == 0 else 3, core)
                cps.append(send(src, dst, xs.at[k, side, e], xr.at[k, side, c], to))
        return cps

    def own_z(act_on):
        for e in range(2):
            core = (c + e) % 2
            src, dst = own_rows(0, core)

            @pl.when(zl < 3)
            def _():
                act_on(send(src, dst, zs_own.at[0, e], zr.at[zl, c], at_zl(zl + 1, core)))

            @pl.when(zl > 0)
            def _():
                act_on(send(src, dst, zs_own.at[1, e], zr.at[zl, c], at_zl(zl - 1, core)))

    def own_core(k, ssem, rsem):
        src, dst = own_rows(k, 1 - c)
        return send(src, dst, ssem, rsem, partner)

    def start(cps):
        for cp in cps:
            cp.start()

    own_z(lambda cp: cp.start())
    start(own_x(0))
    start(own_x(4))
    up_x = own_core(0, up_s, up_r)
    dn_x = own_core(4, dn_s, dn_r)
    start([up_x, dn_x])
    ct = []
    for d in range(1, 8):
        to = (slot + d) % 8
        ct.append(send(ctile.at[slot], ctile.at[slot], ct_s.at[d], ct_r.at[d], at_zl(to // 2, to % 2)))
        ct[-1].start()


    m = zl // 2
    zz = zl + m * (3 - 2 * zl)
    order = [k + m * (3 - 2 * k) for k in (zz, 1 - zz, 2, 3)]

    def rows_of(xp, zp, lo=0, n=ROWS):
        return pl.ds(pl.multiple_of((xp * 4 + zp) * ROWS + lo, 32), n)

    def block(xp, k, lo=0, n=ROWS):
        if k == 4:
            return wdg.at[xp, pl.ds(lo, n), :]
        return wup.at[rows_of(xp, order[k], lo, n), :]

    left, right, far = (x + 3) % 4, (x + 1) % 4, (x + 2) % 4

    def x_half(k, side, h):
        blk = block(x, k, h * 96, 96)
        return send(blk, blk, xs.at[k, side, h], xr.at[k, side, h], at_x(1 if side == 0 else 3))

    def x_out(k):
        return [x_half(k, side, h) for h in range(2) for side in range(2)]

    def x_fwd(k):
        lb, rb = block(left, k, 0, 96), block(right, k, 96, 96)
        return [
            send(lb, lb, xf.at[k, 0], xo.at[k, 0], at_x(1)),
            send(rb, rb, xf.at[k, 1], xo.at[k, 1], at_x(3)),
        ]

    def x_start(k, h):
        x_half(k, h, h).start()
        x_half(k, 1 - h, h).start()

    def x_relay(k):
        fw = x_fwd(k)
        for h, src in enumerate((left, right)):
            blk = block(src, k, h * 96, 96)
            send(blk, blk, xs.at[k, h, h], xr.at[k, h, h], at_x(1)).wait_recv()
            fw[h].start()

    def x_near(k):
        for h, src in enumerate((left, right)):
            blk = block(src, k, 96 - h * 96, 96)
            send(blk, blk, xs.at[k, h, 1 - h], xr.at[k, h, 1 - h], at_x(1)).wait_recv()

    def x_far(k):
        for h in range(2):
            blk = block(far, k, h * 96, 96)
            send(blk, blk, xf.at[k, h], xo.at[k, h], at_x(1)).wait_recv()

    def z_send(k, h, ssem, to):
        blk = block(x, k, h * 96, 96)
        return send(blk, blk, ssem, zr.at[order[k], h], at_zl(to))

    def z_fwd(k, h, act_on):
        zp = order[k]

        @pl.when(jnp.logical_and(zp < zl, zl < 3))
        def _():
            act_on(z_send(k, h, zs_fwd.at[k, h], zl + 1))

        @pl.when(jnp.logical_and(zp > zl, zl > 0))
        def _():
            act_on(z_send(k, h, zs_fwd.at[k, h], zl - 1))

    def z_relay(k, h):
        z_send(k, h, zs_fwd.at[k, h], zl).wait_recv()
        z_fwd(k, h, lambda cp: cp.start())

    def run(*tokens):
        for t in tokens:
            n = [int(v) for v in t[1:]]
            if t[0] == "Z":
                z_relay(*n)
            elif t[0] == "A":
                x_start(*n)
            elif t[0] == "R":
                x_relay(*n)
            elif t[0] == "N":
                x_near(*n)
            elif t[0] == "F":
                x_far(*n)

    cp_ss.wait()

    def mod_cols(i, _):
        cols = pl.ds(pl.multiple_of(i * 512, 512), 512)
        mods[:, cols] = dot(cond_b, wmod[:, cols])
        return 0

    lax.fori_loop(0, 12, mod_cols, 0)
    cp_hid.wait()

    def norm_rows(i, _):
        rows = pl.ds(pl.multiple_of(i * 16, 16), 16)
        v = hid[rows, :].astype(F32)
        mean = jnp.sum(v, axis=1, keepdims=True) * (1.0 / D)
        v = v - mean
        var = jnp.sum(v * v, axis=1, keepdims=True) * (1.0 / D)
        v = v * lax.rsqrt(var + 1e-06)
        v = v * (1.0 + mods[0:1, D:]) + mods[0:1, :D]
        normed[pl.ds(pl.multiple_of(c * TOK + i * 16, 16), 16), :] = v.astype(BF16)
        return 0

    def norm_copy(q):
        rows = pl.ds(pl.multiple_of(c * TOK + q * 96, 32), 96)
        return send(normed.at[rows, :], normed.at[rows, :], nm_s.at[q], nm_r.at[q], partner)

    for q in range(2):
        lax.fori_loop(q * 6, q * 6 + 6, norm_rows, 0)
        norm_copy(q).start()

    run("Z10", "A10", "R0", "Z11", "A11")
    for q in range(2, 4):
        lax.fori_loop(q * 6, q * 6 + 6, norm_rows, 0)
        norm_copy(q).start()
    run("R4")

    cp_out.wait()
    share = pl.ds(pl.multiple_of(te * 384, 128), 384)
    wo = wout[:, share].astype(F32)
    wo = jnp.concatenate([wo, wo], axis=0)
    row = lax.broadcasted_iota(jnp.int32, (128, 384), 0)
    wo = jnp.where(row // 64 == c, wo, 0.0).astype(BF16)
    head[...] = nt_dot(hid[:, share], wo)

    for d in range(1, 8):
        frm = (slot + 8 - d) % 8
        send(ctile.at[frm], ctile.at[frm], ct_s.at[d], ct_r.at[d], partner).wait_recv()
    cp_gate.wait()
    cond8 = ctile[0, :, :TEMB]
    for s in range(1, 8):
        cond8 = cond8 + ctile[s, :, :TEMB]
    cond8 = cond8.astype(BF16)
    for i in range(8):
        g = dot(cond8, wmod[:, 2 * D + i * 384 : 2 * D + (i + 1) * 384])
        gch[2 * i] = g[:, :ROWS]
        gch[2 * i + 1] = g[:, ROWS:]
        wt = wout[:, i * 384 : (i + 1) * 384].astype(F32)
        wch[2 * i] = wt[:, :ROWS]
        wch[2 * i + 1] = wt[:, ROWS:]

    def gate_head(xp, _):
        p = xp * 4 + zl
        wt = wch[p]
        for s in range(8):
            g = gch[p, s : s + 1, :] * wt
            hi = g.astype(BF16)
            gbuf[xp, s * 64 : (s + 1) * 64, :] = hi
            gbuf[xp, 512 + s * 64 : 512 + (s + 1) * 64, :] = (g - hi.astype(F32)).astype(BF16)
        return 0

    lax.fori_loop(0, 4, gate_head, 0)

    run("Z20", "A20", "Z21", "A21", "R1")

    run("Z30", "A30", "Z31", "A31", "N4", "F4")

    def partial(zp, _):
        hi_rows = pl.ds(pl.multiple_of(zp * 128, 128), 128)
        lo_rows = pl.ds(pl.multiple_of(512 + zp * 128, 128), 128)
        acc = jnp.zeros((128, HALF), F32)
        for xp in range(4):
            acc = acc + dot(gbuf[xp, hi_rows, :], wdg[xp]) + dot(gbuf[xp, lo_rows, :], wdg[xp])
        psend[zp] = acc.astype(BF16)

        @pl.when(zp == zl)
        def _():
            pown[...] = acc

        return 0

    cp_dn.wait()
    dn_x.wait_recv()
    lax.fori_loop(0, 4, partial, 0)
    pcopies = []
    for d in (1, 2, 3):
        to = (zl + d) % 4
        pcopies.append(send(psend.at[to], pin.at[zl], ps_s.at[d - 1], ps_r.at[d - 1], at_zl(to)))
        pcopies[-1].start()

    for q in range(4):
        norm_rows_in = pl.ds(pl.multiple_of((1 - c) * TOK + q * 96, 32), 96)
        send(normed.at[norm_rows_in, :], normed.at[norm_rows_in, :], nm_s.at[q], nm_r.at[q], partner).wait_recv()
    run("R2", "N0", "F0", "N1", "F1")

    def chunk(xp, mm):
        return pl.ds(pl.multiple_of((xp * 2 + mm) * 384, 128), 384)

    def up(xps, mm, first):
        def tile_rows(i, _):
            rows = pl.ds(pl.multiple_of(i * 128, 128), 128)
            acc = None if first else pre[rows, :]
            for xp in xps:
                v = dot(normed[rows, chunk(xp, mm)], wup[chunk(xp, mm), :])
                acc = v if acc is None else acc + v
            pre[rows, :] = acc
            return 0

        lax.fori_loop(0, 6, tile_rows, 0)

    cp_up.wait()
    up_x.wait_recv()
    up([x, left, right, far], m, True)
    run("R3", "N2", "N3")
    up([x, left, right], 1 - m, False)

    w2 = pown[...]
    for d in (1, 2, 3):
        frm = (zl + 4 - d) % 4
        send(psend.at[frm], pin.at[frm], ps_s.at[d - 1], ps_r.at[d - 1], at_zl(frm)).wait_recv()
        w2 = w2 + pin[frm].astype(F32)
    hi = w2.astype(BF16)
    lo = (w2 - hi.astype(F32)).astype(BF16)
    w2t[...] = jnp.zeros((256, 768), BF16)
    w2t[0:64, 0:384] = hi[:64]
    w2t[64:128, 384:768] = hi[64:]
    w2t[128:192, 0:384] = lo[:64]
    w2t[192:256, 384:768] = lo[64:]

    lane1 = lax.broadcasted_iota(jnp.int32, (1, 128), 1)
    step0 = jnp.sum(ctile[zl * 2, :, TEMB:], axis=0, keepdims=True)
    step1 = jnp.sum(ctile[zl * 2 + 1, :, TEMB:], axis=0, keepdims=True)
    steps = jnp.where(lane1 < 64, step0, step1)

    run("F2", "F3")

    ya = []
    for d in (2, 1, 3, 0):
        yp = (y + d) % 4
        rows = pl.ds(pl.multiple_of(yp * 96, 32), 96)
        jrows = [pl.ds(pl.multiple_of(j * TOK + yp * 96, 32), 96) for j in range(2)]
        lhs = jnp.concatenate([normed[r, chunk(far, 1 - m)] for r in jrows], axis=0)
        v = dot(lhs, wup[chunk(far, 1 - m), :])
        for j in range(2):
            g = jax.nn.gelu(pre[jrows[j], :] + v[j * 96 : (j + 1) * 96], approximate=True)
            act[:, j * HALF : (j + 1) * HALF] = g.astype(BF16)
        r = nt_dot(act[...], w2t[...])
        tile = (r[:, :128] + r[:, 128:] + head[rows, :]) * steps
        part[yp] = tile.reshape(2, 2, 24, 128)
        for e in range(2):
            if d == 0 and e == 0:
                continue
            core = (c + e) % 2
            n = d * 2 + e
            cp = send(part.at[yp, :, core], ry.at[n], ya_s.at[n], ya_r.at[n], at_y(d, core))
            cp.start()
            ya.append((cp, n))
    tot = part[y, :, c]
    for cp, n in ya:
        cp.wait_recv()
        tot = tot + ry[n]
    rz[...] = tot
    za = []
    for d in range(1, 8):
        to = (z + d) % 8
        za.append(send(rz.at[to // 4], zin.at[z], za_s.at[d - 1], za_r.at[d - 1], at_z(d)))
        za[-1].start()
    zin[z] = rz[zh]
    for d in range(1, 8):
        frm = (z + 8 - d) % 8
        send(rz.at[0], zin.at[frm], za_s.at[d - 1], za_r.at[d - 1], at_z(d)).wait_recv()
    vs = [zin[i] + zin[4 + i] for i in range(4)]
    slide = slide_s[0]
    lane24 = lax.broadcasted_iota(jnp.int32, (24, 128), 1) // 64
    xa = []

    def prefix(xp, cp):
        last = xp * 8 + zl * 2 + cp + slide - 1
        acc = jnp.zeros((24, 128), F32)
        for i in range(4):
            acc = acc + jnp.where(lane24 + (x * 8 + i * 2) <= last, vs[i], 0.0)
        return acc + pltpu.roll(acc, 64, 1)

    for d in range(4):
        for e in range(2):
            if d == 0 and e == 0:
                continue
            n = d * 2 + e
            core = (c + e) % 2
            xsend[n] = prefix((x + d) % 4, core)
            xa.append((send(xsend.at[n], xin.at[x, c], xa_s.at[n], xa_r.at[n], at_x(d, core)), d, e))
            xa[-1][0].start()
    xin[x, c] = prefix(x, c)
    for cp, d, e in xa:
        send(xsend.at[d * 2 + e], xin.at[(x + 4 - d) % 4, (c + e) % 2], xa_s.at[d * 2 + e], xa_r.at[d * 2 + e], partner).wait_recv()
    cp_base.wait()
    for h in range(2):
        s = xin[0, h] + xin[1, h] + xin[2, h] + xin[3, h]
        out_v[h * 24 : (h + 1) * 24, :] = base[h * 24 : (h + 1) * 24, :] + s[:, :64]

    up_x.wait_send()
    dn_x.wait_send()
    for cp in ct + pcopies + za + [t[0] for t in ya + xa]:
        cp.wait_send()
    for q in range(4):
        norm_copy(q).wait_send()
    for k in range(5):
        for cp in (own_x(k) if k in (0, 4) else x_out(k)) + x_fwd(k):
            cp.wait_send()
    own_z(lambda cp: cp.wait_send())
    for h in range(2):
        for k in (1, 2, 3):
            z_fwd(k, h, lambda cp: cp.wait_send())


def body(hidden_state, base_latent, w_modulation, w_up, w_down, w_out, times, sched_index, slide_count):
    hbm = pl.BlockSpec(memory_space=pltpu.HBM)
    V, dma = pltpu.VMEM, pltpu.SemaphoreType.DMA
    out = pl.pallas_call(
        kernel,
        out_shape=jax.ShapeDtypeStruct((48, LAT), F32),
        in_specs=[hbm] * 9,
        out_specs=pl.BlockSpec(memory_space=pltpu.VMEM),
        scratch_shapes=[
            pltpu.SMEM((1,), jnp.int32), pltpu.SMEM((1,), jnp.int32), pltpu.SMEM((1,), jnp.int32),
            V((TOK, D), BF16),
            V((TEMB, 3 * D), BF16),
            V((48, LAT), F32),
            V((LAT, D), BF16),
            V((2 * TOK, D), BF16),
            V((D, HALF), BF16),
            V((4, ROWS, HALF), BF16),
            V((8, 8, TEMB + 128), F32),
            V((8, 2 * D), F32),
            V((16, 8, ROWS), F32),
            V((16, LAT, ROWS), F32),
            V((4, 1024, ROWS), BF16),
            V((4, 128, HALF), BF16),
            V((128, HALF), F32),
            V((4, 128, HALF), BF16),
            V((256, 768), BF16),
            V((2 * TOK, HALF), F32),
            V((96, 2 * HALF), BF16),
            V((TOK, 128), F32),
            V((4, 2, 2, 24, 128), F32),
            V((8, 2, 24, 128), F32),
            V((2, 24, 128), F32),
            V((8, 24, 128), F32),
            V((8, 24, 128), F32),
            V((4, 2, 24, 128), F32),
            dma((10,)),
            dma, dma, dma, dma,
            dma((4,)), dma((4,)),
            dma((8,)), dma((8,)),
            dma((2, 2)), dma((4, 2)), dma((4, 2)),
            dma((5, 2, 2)), dma((5, 2)), dma((5, 2, 2)), dma((5, 2)),
            dma((3,)), dma((3,)),
            dma((8,)), dma((8,)),
            dma((7,)), dma((7,)),
            dma((8,)), dma((8,)),
        ],
        compiler_params=pltpu.CompilerParams(
            collective_id=0, has_side_effects=True, vmem_limit_bytes=56518246
        ),
        cost_estimate=pl.CostEstimate(flops=4 * 10**9, bytes_accessed=10**7, transcendentals=300000),
        name="picard",
    )(
        hidden_state[0], base_latent, w_modulation, w_up, w_down.T, w_out.T,
        times, sched_index, slide_count,
    )
    return out[None]


def solution(mesh):
    placed = (
        P("tm", None, None),
        P("tensor", None),
        P(),
        P("tm", "tensor"),
        P("tensor", "tm"),
        P(),
        P("tm"),
        P("tm"),
        P(),
    )
    return jax.shard_map(
        body, mesh=mesh, in_specs=placed, out_specs=P("tm", "tensor", None), check_vma=False
    )
```

time: 75.2 us -> 56.5 us (0.75)
  Pallas kernels: 65.9 us -> 53.8 us
  local copies, waits for them, and re-layouts: 7.03 us -> 0.61 us
    pallas_call x1, Pallas kernels: 65.9 us -> 53.8 us  [body(): pl.pallas_call(kernel, out_shape=jax.ShapeDtypeStruct((48, LAT), F32), in...]
    unnamed x9 -> x1, local copies, waits for them, and re-layouts: 6.37 us -> 0.61 us
where the time goes in v2:
time: 56.5 us; the launch traced here: 56.4 us
  Pallas kernels  53.8 us (95%)
  between operations  1.95 us (3%)
  local copies, waits for them, and re-layouts  0.61 us (1%)
    pallas_call x1, Pallas kernels, body(): pl.pallas_call(kernel, out_shape=jax.ShapeDtypeStruct((48, LAT), F32), in...  53.8 us

profile of v2, /device:TPU:1, one launch (start us, length us, event | category | flops | bytes accessed | tf_op | source)
XLA Modules:
  0.0 56.4 jit_solution(9687902809886806738)
XLA Ops:
  1.9 53.8 %picard.1 = f32[48,64]{1,0:T(8,128)S(1)} custom-call(bf16[384,3072]{1,0:T(8,128)(2,1)} %bitcast.5, f32[48,64]{1,0:T(8,128)} %base_h.1, bf16[256,9216]{1,0:T(8,128)(2,1)} %wmod_h.1, bf16[96,768]{1,0:T(8,128)(2,1)} %wup_h.1, bf16[96,768]{1,0:T(8,128)(2,1)} %bitcast.7, bf16[64,3072]{1,0:T(8,128)(2,1)} %bitcast.6, s32[1]{0:T(128)S(6)} %copy.11.times_h, ...), custom_call_target="tpu_custom_call" | custom-call | flops 4000000000 | bytes 10000000 | tf_op jit(solution)/shard_map/picard/pallas_call | solution.py:473
  55.8 0.6 %copy.14 = f32[1,48,64]{2,1,0:T(8,128)} copy(f32[1,48,64]{2,1,0:T(8,128)S(1)} %bitcast.4) | data formatting | bytes 24576

commit v3 on v2

--- a/solution.py
+++ b/solution.py
@@ -12,6 +12,14 @@
 D, FFB, LAT, TEMB, TOK = 3072, 768, 64, 256, 384
 HALF = FFB // 2
 ROWS = 192
+VMEM_BYTES = 56518246
+FIRST = (0, 4)
+PLAN = (
+    "M", "K1", "Q0", "Q1", "K2", "C", "Z10", "A10", "R0", "Z11", "A11", "Q2",
+    "Q3", "R4", "H", "G", "Z20", "A20", "Z21", "A21", "R1", "K3", "Z30", "A30",
+    "Z31", "A31", "N4", "F4", "W", "R2", "N0", "F0", "N1", "F1", "U1", "R3",
+    "N2", "N3", "U2", "V", "F2", "F3",
+)
 F32, BF16 = jnp.float32, jnp.bfloat16
 NT = (((1,), (1,)), ((), ()))
 
@@ -33,7 +41,7 @@
     out_v,
     times_s, sched_s, slide_s, hid, wmod, base, wout, normed, wup, wdg, ctile, mods, gch, wch, gbuf, psend, pown, pin,
     w2t, pre, act, head, part, ry, rz, zin, xsend, xin,
-    loc, up_s, up_r, dn_s, dn_r, nm_s, nm_r, ct_s, ct_r, zs_own, zs_fwd, zr, xs, xf, xr, xo,
+    loc, up_s, up_r, dn_s, dn_r, nm_s, nm_r, ct_s, ct_r, ready, zs_own, zs_fwd, zr, xs, xf, xr, xo,
     ps_s, ps_r, ya_s, ya_r, za_s, za_r, xa_s, xa_r,
 ):
     tm, te = lax.axis_index("tm"), lax.axis_index("tensor")
@@ -49,9 +57,9 @@
     def at_zl(zp, core=c):
         return device(x, zp, core, y, zh)
 
-    def at_z(d):
+    def at_z(d, core=c):
         zp = (z + d) % 8
-        return device(x, zp % 4, c, y, zp // 4)
+        return device(x, zp % 4, core, y, zp // 4)
 
     def at_y(d, core=c):
         return device(x, zl, core, (y + d) % 4, zh)
@@ -68,14 +76,12 @@
         pl.semaphore_signal(barrier, inc=1, device_id=dev, device_id_type=pl.DeviceIdType.MESH)
 
     greet(partner)
-    for d in (1, 2, 3):
-        greet(at_x(d))
-        greet(at_x(d, 1 - c))
-        greet(at_y(d))
-        greet(at_y(d, 1 - c))
-        greet(at_zl((zl + d) % 4, 1 - c))
-    for d in range(1, 8):
-        greet(at_z(d))
+    for core in (c, 1 - c):
+        for d in (1, 3):
+            greet(at_x(d, core))
+            greet(at_y(d, core))
+        for d in (1, 7):
+            greet(at_z(d, core))
 
     my_rows = pl.ds(pl.multiple_of(place * ROWS + c * 96, 32), 96)
     mine = pl.ds(pl.multiple_of(c * HALF, 128), HALF)
@@ -105,12 +111,23 @@
     cond = (emb * jax.nn.sigmoid(emb)).astype(BF16).astype(F32)
     step = 0.1 + 0.3 * sched_s[0].astype(F32) / SCHED
     slot = zl * 2 + c
-    tile = jnp.concatenate([cond, jnp.full((8, 128), 1.0, F32) * step], axis=1)
-    rowid = lax.broadcasted_iota(jnp.int32, (8, TEMB + 128), 0)
-    ctile[slot] = jnp.where(rowid == slot, tile, 0.0)
+    ctile[slot] = jnp.concatenate([cond[:1], jnp.full((1, 128), 1.0, F32) * step], axis=1)
     cond_b = cond.astype(BF16)
 
-    pl.semaphore_wait(barrier, 23)
+    pl.semaphore_wait(barrier, 13)
+
+    def tell(n, dev):
+        pl.semaphore_signal(ready.at[n], inc=1, device_id=dev, device_id_type=pl.DeviceIdType.MESH)
+
+    def hear(n):
+        pl.semaphore_wait(ready.at[n], 2)
+        if n < 3:
+            tell(n + 1, at_z(1))
+            tell(n + 1, at_z(7))
+
+    tell(0, at_y(3))
+    tell(1, at_z(1))
+    tell(1, at_z(7))
 
     def own_rows(k, core):
         cols = pl.ds(pl.multiple_of(core * HALF, 128), HALF)
@@ -150,17 +167,22 @@
             cp.start()
 
     own_z(lambda cp: cp.start())
-    start(own_x(0))
-    start(own_x(4))
+    for k in FIRST:
+        start(own_x(k))
     up_x = own_core(0, up_s, up_r)
     dn_x = own_core(4, dn_s, dn_r)
     start([up_x, dn_x])
+    ct_x = send(ctile.at[slot], ctile.at[slot], ct_s.at[0], ct_r.at[0], partner)
+    ct_x.start()
     ct = []
-    for d in range(1, 8):
-        to = (slot + d) % 8
-        ct.append(send(ctile.at[slot], ctile.at[slot], ct_s.at[d], ct_r.at[d], at_zl(to // 2, to % 2)))
-        ct[-1].start()
-
+
+    def share_cond():
+        frm = zl * 2 + 1 - c
+        send(ctile.at[frm], ctile.at[frm], ct_s.at[0], ct_r.at[0], partner).wait_recv()
+        pair = ctile.at[pl.ds(zl * 2, 2)]
+        for d in (1, 2, 3):
+            ct.append(send(pair, pair, ct_s.at[d], ct_r.at[d], at_zl((zl + d) % 4)))
+            ct[-1].start()
 
     m = zl // 2
     zz = zl + m * (3 - 2 * zl)
@@ -230,29 +252,15 @@
         z_send(k, h, zs_fwd.at[k, h], zl).wait_recv()
         z_fwd(k, h, lambda cp: cp.start())
 
-    def run(*tokens):
-        for t in tokens:
-            n = [int(v) for v in t[1:]]
-            if t[0] == "Z":
-                z_relay(*n)
-            elif t[0] == "A":
-                x_start(*n)
-            elif t[0] == "R":
-                x_relay(*n)
-            elif t[0] == "N":
-                x_near(*n)
-            elif t[0] == "F":
-                x_far(*n)
-
-    cp_ss.wait()
-
     def mod_cols(i, _):
         cols = pl.ds(pl.multiple_of(i * 512, 512), 512)
         mods[:, cols] = dot(cond_b, wmod[:, cols])
         return 0
 
-    lax.fori_loop(0, 12, mod_cols, 0)
-    cp_hid.wait()
+    def modulate():
+        cp_ss.wait()
+        lax.fori_loop(0, 12, mod_cols, 0)
+        cp_hid.wait()
 
     def norm_rows(i, _):
         rows = pl.ds(pl.multiple_of(i * 16, 16), 16)
@@ -269,39 +277,18 @@
         rows = pl.ds(pl.multiple_of(c * TOK + q * 96, 32), 96)
         return send(normed.at[rows, :], normed.at[rows, :], nm_s.at[q], nm_r.at[q], partner)
 
-    for q in range(2):
+    def norm(q):
         lax.fori_loop(q * 6, q * 6 + 6, norm_rows, 0)
         norm_copy(q).start()
 
-    run("Z10", "A10", "R0", "Z11", "A11")
-    for q in range(2, 4):
-        lax.fori_loop(q * 6, q * 6 + 6, norm_rows, 0)
-        norm_copy(q).start()
-    run("R4")
-
-    cp_out.wait()
-    share = pl.ds(pl.multiple_of(te * 384, 128), 384)
-    wo = wout[:, share].astype(F32)
-    wo = jnp.concatenate([wo, wo], axis=0)
-    row = lax.broadcasted_iota(jnp.int32, (128, 384), 0)
-    wo = jnp.where(row // 64 == c, wo, 0.0).astype(BF16)
-    head[...] = nt_dot(hid[:, share], wo)
-
-    for d in range(1, 8):
-        frm = (slot + 8 - d) % 8
-        send(ctile.at[frm], ctile.at[frm], ct_s.at[d], ct_r.at[d], partner).wait_recv()
-    cp_gate.wait()
-    cond8 = ctile[0, :, :TEMB]
-    for s in range(1, 8):
-        cond8 = cond8 + ctile[s, :, :TEMB]
-    cond8 = cond8.astype(BF16)
-    for i in range(8):
-        g = dot(cond8, wmod[:, 2 * D + i * 384 : 2 * D + (i + 1) * 384])
-        gch[2 * i] = g[:, :ROWS]
-        gch[2 * i + 1] = g[:, ROWS:]
-        wt = wout[:, i * 384 : (i + 1) * 384].astype(F32)
-        wch[2 * i] = wt[:, :ROWS]
-        wch[2 * i + 1] = wt[:, ROWS:]
+    def head_share():
+        cp_out.wait()
+        share = pl.ds(pl.multiple_of(te * 384, 128), 384)
+        wo = wout[:, share].astype(F32)
+        wo = jnp.concatenate([wo, wo], axis=0)
+        row = lax.broadcasted_iota(jnp.int32, (128, 384), 0)
+        wo = jnp.where(row // 64 == c, wo, 0.0).astype(BF16)
+        head[...] = nt_dot(hid[:, share], wo)
 
     def gate_head(xp, _):
         p = xp * 4 + zl
@@ -313,11 +300,24 @@
             gbuf[xp, 512 + s * 64 : 512 + (s + 1) * 64, :] = (g - hi.astype(F32)).astype(BF16)
         return 0
 
-    lax.fori_loop(0, 4, gate_head, 0)
-
-    run("Z20", "A20", "Z21", "A21", "R1")
-
-    run("Z30", "A30", "Z31", "A31", "N4", "F4")
+    def gates():
+        for d in (1, 2, 3):
+            pair = ctile.at[pl.ds((zl + 4 - d) % 4 * 2, 2)]
+            send(pair, pair, ct_s.at[d], ct_r.at[d], partner).wait_recv()
+        cp_gate.wait()
+        row8 = lax.broadcasted_iota(jnp.int32, (8, TEMB), 0)
+        cond8 = jnp.zeros((8, TEMB), F32)
+        for s in range(8):
+            cond8 = jnp.where(row8 == s, ctile[s, :, :TEMB], cond8)
+        cond8 = cond8.astype(BF16)
+        for i in range(8):
+            g = dot(cond8, wmod[:, 2 * D + i * 384 : 2 * D + (i + 1) * 384])
+            gch[2 * i] = g[:, :ROWS]
+            gch[2 * i + 1] = g[:, ROWS:]
+            wt = wout[:, i * 384 : (i + 1) * 384].astype(F32)
+            wch[2 * i] = wt[:, :ROWS]
+            wch[2 * i + 1] = wt[:, ROWS:]
+        lax.fori_loop(0, 4, gate_head, 0)
 
     def partial(zp, _):
         hi_rows = pl.ds(pl.multiple_of(zp * 128, 128), 128)
@@ -333,19 +333,17 @@
 
         return 0
 
-    cp_dn.wait()
-    dn_x.wait_recv()
-    lax.fori_loop(0, 4, partial, 0)
     pcopies = []
-    for d in (1, 2, 3):
-        to = (zl + d) % 4
-        pcopies.append(send(psend.at[to], pin.at[zl], ps_s.at[d - 1], ps_r.at[d - 1], at_zl(to)))
-        pcopies[-1].start()
-
-    for q in range(4):
-        norm_rows_in = pl.ds(pl.multiple_of((1 - c) * TOK + q * 96, 32), 96)
-        send(normed.at[norm_rows_in, :], normed.at[norm_rows_in, :], nm_s.at[q], nm_r.at[q], partner).wait_recv()
-    run("R2", "N0", "F0", "N1", "F1")
+
+    def fold():
+
+        cp_dn.wait()
+        dn_x.wait_recv()
+        lax.fori_loop(0, 4, partial, 0)
+        for d in (1, 2, 3):
+            to = (zl + d) % 4
+            pcopies.append(send(psend.at[to], pin.at[zl], ps_s.at[d - 1], ps_r.at[d - 1], at_zl(to)))
+            pcopies[-1].start()
 
     def chunk(xp, mm):
         return pl.ds(pl.multiple_of((xp * 2 + mm) * 384, 128), 384)
@@ -362,32 +360,60 @@
 
         lax.fori_loop(0, 6, tile_rows, 0)
 
-    cp_up.wait()
-    up_x.wait_recv()
-    up([x, left, right, far], m, True)
-    run("R3", "N2", "N3")
-    up([x, left, right], 1 - m, False)
-
-    w2 = pown[...]
-    for d in (1, 2, 3):
-        frm = (zl + 4 - d) % 4
-        send(psend.at[frm], pin.at[frm], ps_s.at[d - 1], ps_r.at[d - 1], at_zl(frm)).wait_recv()
-        w2 = w2 + pin[frm].astype(F32)
-    hi = w2.astype(BF16)
-    lo = (w2 - hi.astype(F32)).astype(BF16)
-    w2t[...] = jnp.zeros((256, 768), BF16)
-    w2t[0:64, 0:384] = hi[:64]
-    w2t[64:128, 384:768] = hi[64:]
-    w2t[128:192, 0:384] = lo[:64]
-    w2t[192:256, 384:768] = lo[64:]
+    def up_first():
+        for q in range(4):
+            norm_rows_in = pl.ds(pl.multiple_of((1 - c) * TOK + q * 96, 32), 96)
+            send(normed.at[norm_rows_in, :], normed.at[norm_rows_in, :], nm_s.at[q], nm_r.at[q], partner).wait_recv()
+        cp_up.wait()
+        up_x.wait_recv()
+        up([x, left, right, far], m, True)
+
+    def up_second():
+        up([x, left, right], 1 - m, False)
+
+    def collect():
+        w2 = pown[...]
+        for d in (1, 2, 3):
+            frm = (zl + 4 - d) % 4
+            send(psend.at[frm], pin.at[frm], ps_s.at[d - 1], ps_r.at[d - 1], at_zl(frm)).wait_recv()
+            w2 = w2 + pin[frm].astype(F32)
+        hi = w2.astype(BF16)
+        lo = (w2 - hi.astype(F32)).astype(BF16)
+        w2t[...] = jnp.zeros((256, 768), BF16)
+        w2t[0:64, 0:384] = hi[:64]
+        w2t[64:128, 384:768] = hi[64:]
+        w2t[128:192, 0:384] = lo[:64]
+        w2t[192:256, 384:768] = lo[64:]
+
+    work = {
+        "M": modulate, "Q0": norm, "Q1": norm, "Q2": norm, "Q3": norm, "H": head_share,
+        "C": share_cond, "K1": hear, "K2": hear, "K3": hear, "G": gates, "W": fold, "U1": lambda _: up_first(), "U2": lambda _: up_second(), "V": collect,
+    }
+
+    def run(*tokens):
+        for t in tokens:
+            n = [int(v) for v in t[1:]]
+            if t[0] == "Z":
+                z_relay(*n)
+            elif t in work:
+                work[t](*n)
+            elif t[0] == "A":
+                x_start(*n)
+            elif t[0] == "R":
+                x_relay(*n)
+            elif t[0] == "N":
+                x_near(*n)
+            elif t[0] == "F":
+                x_far(*n)
+
+    run(*PLAN)
 
     lane1 = lax.broadcasted_iota(jnp.int32, (1, 128), 1)
-    step0 = jnp.sum(ctile[zl * 2, :, TEMB:], axis=0, keepdims=True)
-    step1 = jnp.sum(ctile[zl * 2 + 1, :, TEMB:], axis=0, keepdims=True)
+    step0 = ctile[zl * 2, :, TEMB:]
+    step1 = ctile[zl * 2 + 1, :, TEMB:]
     steps = jnp.where(lane1 < 64, step0, step1)
 
-    run("F2", "F3")
-
+    pl.semaphore_wait(ready.at[0], 1)
     ya = []
     for d in (2, 1, 3, 0):
         yp = (y + d) % 4
@@ -452,6 +478,7 @@
         s = xin[0, h] + xin[1, h] + xin[2, h] + xin[3, h]
         out_v[h * 24 : (h + 1) * 24, :] = base[h * 24 : (h + 1) * 24, :] + s[:, :64]
 
+    ct_x.wait_send()
     up_x.wait_send()
     dn_x.wait_send()
     for cp in ct + pcopies + za + [t[0] for t in ya + xa]:
@@ -484,7 +511,7 @@
             V((2 * TOK, D), BF16),
             V((D, HALF), BF16),
             V((4, ROWS, HALF), BF16),
-            V((8, 8, TEMB + 128), F32),
+            V((8, 1, TEMB + 128), F32),
             V((8, 2 * D), F32),
             V((16, 8, ROWS), F32),
             V((16, LAT, ROWS), F32),
@@ -505,7 +532,8 @@
             dma((10,)),
             dma, dma, dma, dma,
             dma((4,)), dma((4,)),
-            dma((8,)), dma((8,)),
+            dma((4,)), dma((4,)),
+            pltpu.SemaphoreType.REGULAR((4,)),
             dma((2, 2)), dma((4, 2)), dma((4, 2)),
             dma((5, 2, 2)), dma((5, 2)), dma((5, 2, 2)), dma((5, 2)),
             dma((3,)), dma((3,)),
@@ -514,7 +542,7 @@
             dma((8,)), dma((8,)),
         ],
         compiler_params=pltpu.CompilerParams(
-            collective_id=0, has_side_effects=True, vmem_limit_bytes=56518246
+            collective_id=0, has_side_effects=True, vmem_limit_bytes=VMEM_BYTES
         ),
         cost_estimate=pl.CostEstimate(flops=4 * 10**9, bytes_accessed=10**7, transcendentals=300000),
         name="picard",

time: 56.5 us -> 55.6 us (0.984)
  Pallas kernels: 53.8 us -> 53 us
    pallas_call x1, Pallas kernels: 53.8 us -> 53 us  [body(): pl.pallas_call(kernel, out_shape=jax.ShapeDtypeStruct((48, LAT), F32), in...]
where the time goes in v3:
time: 55.6 us; the launch traced here: 55.5 us
  Pallas kernels  53 us (95%)
  between operations  1.95 us (4%)
  local copies, waits for them, and re-layouts  0.61 us (1%)
    pallas_call x1, Pallas kernels, body(): pl.pallas_call(kernel, out_shape=jax.ShapeDtypeStruct((48, LAT), F32), in...  53 us

profile of v3, /device:TPU:1, one launch (start us, length us, event | category | flops | bytes accessed | tf_op | source)
XLA Modules:
  0.0 55.5 jit_solution(4219101898781668844)
XLA Ops:
  1.9 53.0 %picard.1 = f32[48,64]{1,0:T(8,128)S(1)} custom-call(bf16[384,3072]{1,0:T(8,128)(2,1)} %bitcast.5, f32[48,64]{1,0:T(8,128)} %base_h.1, bf16[256,9216]{1,0:T(8,128)(2,1)} %wmod_h.1, bf16[96,768]{1,0:T(8,128)(2,1)} %wup_h.1, bf16[96,768]{1,0:T(8,128)(2,1)} %bitcast.7, bf16[64,3072]{1,0:T(8,128)(2,1)} %bitcast.6, s32[1]{0:T(128)S(6)} %copy.11.times_h, ...), custom_call_target="tpu_custom_call" | custom-call | flops 4000000000 | bytes 10000000 | tf_op jit(solution)/shard_map/picard/pallas_call | solution.py:500
  54.9 0.6 %copy.14 = f32[1,48,64]{2,1,0:T(8,128)} copy(f32[1,48,64]{2,1,0:T(8,128)S(1)} %bitcast.4) | data formatting | bytes 24576
